TPU v7x, 512 devices: a whole 4x8x8 slice. The times are simulated.
512 devices in a mesh: ax: 32 (over x, z), tr: 16 (over y, core).
Axes of the slice: x: 4, y: 8, z: 8, core: 2. Of those that a mesh axis runs over, the one named last changes fastest.
Arguments:
- solid_start: bfloat16 [64, 1024, 4096], P(None, 'ax', 'tr'), may hold values from -80 to 80
- inlet: float32 [64, 4096], P(None, 'tr'), may hold values from -4 to 4
- ntu: float32 [1024, 4096], P('ax', 'tr'), may hold values from 0 to 1
- solid_rate: float32 [1024, 4096], P('ax', 'tr'), may hold values from 0.2 to 0.8
Outputs:
- basis: float32 [64, 2, 1024, 4096], P(None, None, 'ax', 'tr')
- factor: float32 [64, 64], replicated
All inputs are finite; a program needn't handle non-finite values.
Results may differ from a plain program's by a relative error of at most 0.0003.
Values sent between devices are 32-bit elements; how exact they have to be, the bound alone decides.
A program may use at most 128 MiB of HBM per device.

v0:
```python
import jax
import jax.numpy as jnp
from jax import lax
from jax.sharding import PartitionSpec as P

STEPS = 2


def prefix(value, axis, join, neutral):
    count, mine = (lax.axis_size(axis), lax.axis_index(axis))
    pieces = jax.tree.map(lambda part: lax.all_gather(part, axis), value)
    subtotal = jax.tree.map(
        lambda part, zero: jnp.full_like(part, 0) + jnp.asarray(zero, part.dtype), value, neutral
    )

    def step(position, subtotal):
        longer = join(subtotal, jax.tree.map(lambda part: part[position], pieces))
        return jax.tree.map(lambda new, old: jnp.where(position < mine, new, old), longer, subtotal)

    return lax.fori_loop(0, count - 1, step, subtotal)


def compose(earlier, later):
    return (later[0] * earlier[0], later[0] * earlier[1] + later[1])


def per_device(solid_start, inlet, ntu, solid_rate):
    columns = solid_start.shape[0]
    cells = solid_start.shape[2]
    carry_coef = 1.0 / (1.0 + ntu)
    source_coef = ntu / (1.0 + ntu)
    solid_temp = solid_start.astype(jnp.float32)
    fluid_temp = solid_temp
    for repeat in range(STEPS):
        source_terms = source_coef[None] * solid_temp
        prefix_scale, prefix_shift = lax.associative_scan(
            compose, (carry_coef[None], source_terms), axis=1
        )
        block_scale = prefix_scale[0, -1]
        block_shift = prefix_shift[:, -1]
        identity = (jnp.ones((cells,), jnp.float32), jnp.zeros((columns, cells), jnp.float32))
        enter_scale, enter_shift = prefix((block_scale, block_shift), "ax", compose, identity)
        entering = enter_scale[None, :] * inlet + enter_shift
        fluid_temp = prefix_scale * entering[:, None, :] + prefix_shift
        solid_temp = solid_temp + solid_rate[None] * (fluid_temp - solid_temp)
    local_gram = jnp.einsum("nzt,mzt->nm", fluid_temp, fluid_temp, precision=lax.Precision.HIGHEST)
    local_gram = local_gram + jnp.einsum(
        "nzt,mzt->nm", solid_temp, solid_temp, precision=lax.Precision.HIGHEST
    )
    gram_matrix = lax.psum(local_gram, ("ax", "tr"))
    lower_factor = jnp.linalg.cholesky(gram_matrix)
    total_rows = 2 * solid_start.shape[1] * lax.axis_size("ax") * cells * lax.axis_size("tr")
    root_rows = jnp.sqrt(jnp.float32(total_rows))
    inverse = lax.linalg.triangular_solve(
        lower_factor, jnp.eye(columns, dtype=jnp.float32), left_side=True, lower=True
    )
    fluid_basis = jnp.einsum("nm,mzt->nzt", inverse, fluid_temp, precision=lax.Precision.HIGHEST)
    solid_basis = jnp.einsum("nm,mzt->nzt", inverse, solid_temp, precision=lax.Precision.HIGHEST)
    basis = jnp.stack([fluid_basis, solid_basis], axis=1) * root_rows
    factor = lower_factor.T / root_rows
    return (basis, factor)


def solution(mesh):
    placed = (P(None, "ax", "tr"), P(None, "tr"), P("ax", "tr"), P("ax", "tr"))
    return jax.shard_map(
        per_device,
        mesh=mesh,
        in_specs=placed,
        out_specs=(P(None, None, "ax", "tr"), P()),
        check_vma=False,
    )
```

profile of v0, /device:TPU:1, one launch (start us, length us, event | category | flops | bytes accessed | tf_op | source)
XLA Modules:
  0.0 493.2 jit_solution(988578101827555497)
XLA Ops:
  8.9 1.9 convert_multiply_fusion
  15.2 0.9 pad.115
  16.1 2.2 pad.116
  18.3 1.7 add.273
  20.0 1.1 fusion.9
  21.1 2.1 pad.117
  23.2 3.7 pad.118
  26.9 2.1 add.275
  29.0 1.3 fusion.7
  31.1 3.5 pad.119
  34.6 5.7 %pad.120 = f32[64,16,256]{2,0,1:T(8,128)} pad(f32[64,8,256]{2,0,1:T(8,128)} %add.275, f32[]{:T(128)} %constant.94.clone.1), padding=0_0_0x1_0_1x0_0_0 | pad | bytes 1572868 | tf_op jit(solution)/shard_map/pad | solution.py:36
  40.3 2.4 add.277
  44.0 10.2 %pad.122 = f32[64,32,256]{2,0,1:T(8,128)} pad(f32[64,16,256]{2,0,1:T(8,128)} %add.277, f32[]{:T(128)} %constant.94.clone.1), padding=0_0_0x1_0_1x0_0_0 | pad | bytes 3145732 | tf_op jit(solution)/shard_map/pad | solution.py:36
  54.3 1.5 slice_add_fusion.10
  57.6 40.6 %all-gather = f32[32,1,256]{2,1,0:T(1,128)S(1)} all-gather(f32[1,1,256]{2,1,0:T(1,128)S(1)} %slice_add_fusion.12), channel_id=2, replica_groups=mesh['ax'=32,'tr'=16] {'ax'}, dimensions={0}, use_global_device_ids=true | all-gather | bytes 33792 | tf_op jit(solution)/shard_map/all_gather | solution.py:11
  98.2 43.2 %all-gather.6.cloned.1.call-done = f32[2048,1,256]{2,0,1:T(8,128)} async-done(((f32[64,1,256]{2,0,1:T(8,128)}), f32[2048,1,256]{2,0,1:T(8,128)}) %all-gather.6.cloned.1.call-update) | async-done | bytes 2097168 | tf_op jit(solution)/shard_map/all_gather | solution.py:11
  141.4 28.6 %while.32 = (s32[]{:T(128)}, f32[256]{0:T(256)S(1)}, f32[64,256]{1,0:T(8,128)S(1)}, s32[]{:T(128)}, f32[32,256]{1,0:T(8,128)S(1)}, /*index=5*/f32[32,64,256]{2,1,0:T(8,128)}, s32[]{:T(128)}, s32[]{:T(128)}) while((s32[]{:T(128)}, f32[256]{0:T(256)S(1)}, f32[64,256]{1,0:T(8,128)S(1)}, s32[]{:T(128)}, f32[32,256]{1,0:T(8,128)S(1)}, ...), condition=%wide.region_1.2_spmd.clone, body=%wide.region_0.1_spmd.clone.sunk | while | flops 66308 | bytes 202875 | solution.py:20
  142.3 0.9 fusion.32
  143.2 0.9 fusion.32
  144.2 0.9 fusion.32
  145.1 0.9 fusion.32
  146.0 0.9 fusion.32
  146.9 0.9 fusion.32
  147.9 0.9 fusion.32
  148.8 0.9 fusion.32
  149.7 0.9 fusion.32
  150.6 0.9 fusion.32
  151.6 0.9 fusion.32
  152.5 0.9 fusion.32
  153.4 0.9 fusion.32
  154.3 0.9 fusion.32
  155.3 0.9 fusion.32
  156.2 0.9 fusion.32
  157.1 0.9 fusion.32
  160.8 0.9 fusion.32
  166.4 0.9 fusion.32
  170.1 4.6 broadcast_multiply_fusion
  178.5 0.9 pad.125
  179.4 2.2 pad.126
  181.7 1.1 fusion.8
  182.7 1.7 add.290
  184.5 2.1 pad.127
  186.6 3.8 pad.128
  190.3 1.3 fusion.6
  193.5 3.5 pad.129
  197.0 5.8 %pad.130 = f32[64,16,256]{2,0,1:T(8,128)} pad(f32[64,8,256]{2,0,1:T(8,128)} %add.292, f32[]{:T(128)} %constant.94.clone.1), padding=0_0_0x1_0_1x0_0_0 | pad | bytes 1572868 | tf_op jit(solution)/shard_map/pad | solution.py:36
  202.8 1.5 fusion.4
  204.3 1.2 add.294
  205.5 1.1 pad_maximum_fusion.1
  206.5 7.0 %pad.131 = f32[64,32,256]{2,0,1:T(8,128)S(1)} pad(f32[64,16,256]{2,0,1:T(8,128)} %pad_maximum_fusion.1, f32[]{:T(128)} %constant.94.clone.1), padding=0_0_0x0_1_1x0_0_0 | pad | bytes 3145732 | tf_op jit(solution)/shard_map/pad | solution.py:36
  213.6 6.3 %pad.132 = f32[64,32,256]{2,0,1:T(8,128)} pad(f32[64,16,256]{2,0,1:T(8,128)S(1)} %copy-done.8, f32[]{:T(128)} %constant.94.clone.1), padding=0_0_0x1_0_1x0_0_0 | pad | bytes 3145732 | tf_op jit(solution)/shard_map/pad | solution.py:36
  219.9 1.5 slice_add_fusion.8
  221.4 80.9 %all-gather.8.cloned.1.call-done = f32[2048,1,256]{2,0,1:T(8,128)} async-done(((f32[64,1,256]{2,0,1:T(8,128)}), f32[2048,1,256]{2,0,1:T(8,128)}) %all-gather.8.cloned.1.call-update) | async-done | bytes 2097168 | tf_op jit(solution)/shard_map/all_gather | solution.py:11
  302.4 49.7 %while.33 = (s32[]{:T(128)}, f32[256]{0:T(256)S(1)}, f32[64,256]{1,0:T(8,128)S(1)}, s32[]{:T(128)}, f32[32,256]{1,0:T(8,128)}, /*index=5*/f32[32,64,256]{2,1,0:T(8,128)}, s32[]{:T(128)}, s32[]{:T(128)}) while((s32[]{:T(128)}, f32[256]{0:T(256)S(1)}, f32[64,256]{1,0:T(8,128)S(1)}, s32[]{:T(128)}, f32[32,256]{1,0:T(8,128)}, ...), condition=%wide.region_3.4_spmd.clone, body=%wide.region_2.3_spmd.clone.sunk | while | flops 66308 | bytes 202875 | solution.py:20
  352.1 2.8 multiply_add_fusion.1
  355.0 1.9 convolution_bitcast_fusion.3
  356.9 1.8 fusion.3
  358.7 99.3 %psum.7 = f32[64,64]{0,1:T(8,128)S(1)} all-reduce(f32[64,64]{0,1:T(8,128)S(1)} %fusion.3), channel_id=1, replica_groups=mesh['ax'=32,'tr'=16] {'ax','tr'}, use_global_device_ids=true, to_apply=%region_4.5 | all-reduce | flops 4096 | bytes 32768 | tf_op jit(solution)/shard_map/psum | solution.py:50
  458.2 5.8 %cholesky.17 = f32[64,64]{1,0:T(8,128)S(1)} custom-call(f32[64,64]{1,0:T(8,128)S(1)} %fusion.18), custom_call_target="Cholesky" | custom-call | tf_op jit(solution)/shard_map/jit(cholesky)/cholesky | solution.py:51
  465.4 4.9 custom-call.6
  470.5 4.9 convolution_bitcast_fusion
  475.4 3.2 convolution_bitcast_fusion.1
  479.3 2.6 maximum_multiply_fusion
  481.9 4.4 copy.27
  (358 shorter events, 77.8 us)
Async XLA Ops:
  7.2 134.2 %all-gather.6.cloned.1.call-start = ((), (), s32[]{:S(2)}) async-start(), calls=%async_computation | async-start | bytes 2162688 | tf_op jit(solution)/shard_map/all_gather | solution.py:11
  8.0 0.9 copy-start.23
  8.0 34.7 %copy-start.14 = (f32[1,15,256]{2,1,0:T(8,128)}, f32[1,15,256]{2,1,0:T(8,128)S(1)}, u32[]{:S(2)}) copy-start(f32[1,15,256]{2,1,0:T(8,128)S(1)} %slice.254) | copy-start | bytes 46084
  8.1 0.8 copy-start.29
  8.1 4.2 copy-start.24
  8.1 20.9 %copy-start.26 = (f32[1,7,256]{2,1,0:T(8,128)}, f32[1,7,256]{2,1,0:T(8,128)S(1)}, u32[]{:S(2)}) copy-start(f32[1,7,256]{2,1,0:T(8,128)S(1)} %slice.258) | copy-start | bytes 21508
  8.2 3.5 copy-start.36
  8.2 4.2 copy-start.30
  8.9 5.0 %copy-start.37 = (f32[1,2,256]{2,1,0:T(2,128)}, f32[1,2,256]{2,1,0:T(2,128)S(1)}, u32[]{:S(2)}) copy-start(f32[1,2,256]{2,1,0:T(2,128)S(1)} %slice.267) | copy-start | bytes 6148
  8.9 4.3 copy-start.43
  8.9 4.3 copy-start.45
  8.9 4.9 copy-start.39
  12.4 0.8 copy-start.9
  12.4 7.6 %copy-start.32 = (f32[1,3,256]{2,1,0:T(4,128)S(1)}, f32[1,3,256]{2,1,0:T(4,128)}, u32[]{:S(2)}) copy-start(f32[1,3,256]{2,1,0:T(4,128)} %slice.262) | copy-start | bytes 9220
  13.2 7.9 %slice-start = ((f32[64,8,256]{2,0,1:T(8,128)}), f32[64,1,256]{2,0,1:T(8,128)S(1)}, s32[]{:S(2)}) async-start(f32[64,8,256]{2,0,1:T(8,128)} %copy-done.9), calls=%async_computation.2 | async-start | bytes 131072 | tf_op jit(solution)/shard_map/slice | solution.py:36
  13.8 7.3 %copy-start.41 = (f32[1,1,256]{2,1,0:T(1,128)}, f32[1,1,256]{2,1,0:T(1,128)S(1)}, u32[]{:S(2)}) copy-start(f32[1,1,256]{2,1,0:T(1,128)S(1)} %get-tuple-element.314) | copy-start | bytes 3076
  23.2 7.1 %copy-start.22 = (f32[64,1,256]{2,0,1:T(8,128)S(1)}, f32[64,1,256]{2,0,1:T(8,128)}, u32[]{:S(2)}) copy-start(f32[64,1,256]{2,0,1:T(8,128)} %slice.340) | copy-start | bytes 196612
  40.3 2.4 copy-start.2
  42.7 0.8 copy-start.20
  43.9 97.5 %copy-start.4 = (f32[64,32,256]{2,0,1:T(8,128)}, f32[64,32,256]{2,0,1:T(8,128)S(1)}, u32[]{:S(2)}) copy-start(f32[64,32,256]{2,0,1:T(8,128)S(1)} %pad.121) | copy-start | bytes 6291460
  43.9 13.3 %copy-start.47 = (f32[1,1,256]{2,1,0:T(1,128)S(1)}, f32[1,1,256]{2,1,0:T(1,128)}, u32[]{:S(2)}) copy-start(f32[1,1,256]{2,1,0:T(1,128)} %get-tuple-element.312) | copy-start | bytes 3076
  43.9 13.3 %copy-start.48 = (f32[1,1,256]{2,1,0:T(1,128)S(1)}, f32[1,1,256]{2,1,0:T(1,128)}, u32[]{:S(2)}) copy-start(f32[1,1,256]{2,1,0:T(1,128)} %get-tuple-element.313) | copy-start | bytes 3076
  44.0 13.3 %copy-start.44 = (f32[1,1,256]{2,1,0:T(1,128)S(1)}, f32[1,1,256]{2,1,0:T(1,128)}, u32[]{:S(2)}) copy-start(f32[1,1,256]{2,1,0:T(1,128)} %copy-done.43) | copy-start | bytes 3076
  44.0 13.3 %copy-start.46 = (f32[1,1,256]{2,1,0:T(1,128)S(1)}, f32[1,1,256]{2,1,0:T(1,128)}, u32[]{:S(2)}) copy-start(f32[1,1,256]{2,1,0:T(1,128)} %copy-done.45) | copy-start | bytes 3076
  44.0 13.3 %copy-start.33 = (f32[1,3,256]{2,1,0:T(4,128)S(1)}, f32[1,3,256]{2,1,0:T(4,128)}, u32[]{:S(2)}) copy-start(f32[1,3,256]{2,1,0:T(4,128)} %slice.262) | copy-start | bytes 9220
  44.0 13.3 %slice-start.2 = ((f32[1,8,256]{2,1,0:T(8,128)}), f32[1,1,256]{2,1,0:T(1,128)S(1)}, s32[]{:S(2)}) async-start(f32[1,8,256]{2,1,0:T(8,128)} %copy-done.36), calls=%async_computation.4 | async-start | bytes 2048 | tf_op jit(solution)/shard_map/slice | solution.py:36
  44.0 13.4 %copy-start.27 = (f32[1,7,256]{2,1,0:T(8,128)S(1)}, f32[1,7,256]{2,1,0:T(8,128)}, u32[]{:S(2)}) copy-start(f32[1,7,256]{2,1,0:T(8,128)} %copy-done.26) | copy-start | bytes 21508
  44.0 13.5 %copy-start.15 = (f32[1,15,256]{2,1,0:T(8,128)S(1)}, f32[1,15,256]{2,1,0:T(8,128)}, u32[]{:S(2)}) copy-start(f32[1,15,256]{2,1,0:T(8,128)} %copy-done.14) | copy-start | bytes 46084
  44.0 126.0 %copy-start.17 = (f32[64,256]{1,0:T(8,128)S(1)}, f32[64,256]{1,0:T(8,128)}, u32[]{:S(2)}) copy-start(f32[64,256]{1,0:T(8,128)} %param.9) | copy-start | bytes 196612
  44.0 126.0 %copy-start.7 = (bf16[64,32,256]{2,1,0:T(8,128)(2,1)S(1)}, bf16[64,32,256]{2,1,0:T(8,128)(2,1)}, u32[]{:S(2)}) copy-start(bf16[64,32,256]{2,1,0:T(8,128)(2,1)} %param.8) | copy-start | bytes 3145732
  44.0 126.0 %copy-start.11 = (f32[32,256]{1,0:T(8,128)S(1)}, f32[32,256]{1,0:T(8,128)}, u32[]{:S(2)}) copy-start(f32[32,256]{1,0:T(8,128)} %param.11) | copy-start | bytes 98308
  55.7 246.6 %all-gather.8.cloned.1.call-start = ((), (), s32[]{:S(2)}) async-start(), calls=%async_computation.1 | async-start | bytes 2162688 | tf_op jit(solution)/shard_map/all_gather | solution.py:11
  98.2 76.5 %copy-start.12 = (f32[32,256]{1,0:T(8,128)}, f32[32,256]{1,0:T(8,128)S(1)}, u32[]{:S(2)}) copy-start(f32[32,256]{1,0:T(8,128)S(1)} %add_bitcast_fusion) | copy-start | bytes 98308
  170.0 4.7 copy-start.35
  174.7 1.5 copy-start.25
  175.3 1.7 copy-start.31
  175.5 1.6 copy-start.38
  175.5 1.6 copy-start.40
  175.5 1.7 copy-start.42
  176.2 5.5 %copy-start.34 = (f32[1,3,256]{2,1,0:T(4,128)S(1)}, f32[1,3,256]{2,1,0:T(4,128)}, u32[]{:S(2)}) copy-start(f32[1,3,256]{2,1,0:T(4,128)} %slice.262) | copy-start | bytes 9220
  176.2 0.8 copy-start.10
  177.1 7.3 %slice-start.1 = ((f32[64,8,256]{2,0,1:T(8,128)}), f32[64,1,256]{2,0,1:T(8,128)S(1)}, s32[]{:S(2)}) async-start(f32[64,8,256]{2,0,1:T(8,128)} %copy-done.10), calls=%async_computation.3 | async-start | bytes 131072 | tf_op jit(solution)/shard_map/slice | solution.py:36
  179.4 10.9 %copy-start.28 = (f32[1,7,256]{2,1,0:T(8,128)S(1)}, f32[1,7,256]{2,1,0:T(8,128)}, u32[]{:S(2)}) copy-start(f32[1,7,256]{2,1,0:T(8,128)} %copy-done.26) | copy-start | bytes 21508
  186.6 6.1 %copy-start.21 = (f32[64,1,256]{2,0,1:T(8,128)S(1)}, f32[64,1,256]{2,0,1:T(8,128)}, u32[]{:S(2)}) copy-start(f32[64,1,256]{2,0,1:T(8,128)} %slice.357) | copy-start | bytes 196612
  190.3 1.4 copy-start.5
  190.3 1.5 copy-start.6
  192.7 10.1 %copy-start.16 = (f32[1,15,256]{2,1,0:T(8,128)S(1)}, f32[1,15,256]{2,1,0:T(8,128)}, u32[]{:S(2)}) copy-start(f32[1,15,256]{2,1,0:T(8,128)} %copy-done.14) | copy-start | bytes 46084
  202.8 1.5 copy-start.1
  204.3 1.2 copy-start.19
  206.5 7.0 %copy-start.8 = (f32[64,16,256]{2,0,1:T(8,128)S(1)}, f32[64,16,256]{2,0,1:T(8,128)}, u32[]{:S(2)}) copy-start(f32[64,16,256]{2,0,1:T(8,128)} %add.294) | copy-start | bytes 3145732
  213.6 88.8 %copy-start.3 = (f32[64,32,256]{2,0,1:T(8,128)}, f32[64,32,256]{2,0,1:T(8,128)S(1)}, u32[]{:S(2)}) copy-start(f32[64,32,256]{2,0,1:T(8,128)S(1)} %pad.131) | copy-start | bytes 6291460
  213.6 138.5 %copy-start.18 = (f32[64,256]{1,0:T(8,128)S(1)}, f32[64,256]{1,0:T(8,128)}, u32[]{:S(2)}) copy-start(f32[64,256]{1,0:T(8,128)} %param.9) | copy-start | bytes 196612
  213.6 138.5 %copy-start.13 = (f32[32,256]{1,0:T(8,128)S(1)}, f32[32,256]{1,0:T(8,128)}, u32[]{:S(2)}) copy-start(f32[32,256]{1,0:T(8,128)} %copy-done.12) | copy-start | bytes 98308
  352.1 2.9 copy-start
Sparse Core Ops, SparseCore 0:
  55.9 85.4 all-gather.5
  221.5 80.7 all-gather.7
where the time goes:
time: 500 us; the launch traced here: 493 us
  blocking collectives  140 us (28%)
  waiting for transfers between devices  124 us (25%)
  other arithmetic  105 us (21%)
  local copies, waits for them, and re-layouts  95 us (19%)
  between operations  14.9 us (3%)
  matrix products  12.1 us (2%)
    all_gather x2, waiting for transfers between devices, prefix(): pieces = jax.tree.map(lambda part: lax.all_gather(part, axis), value)  124 us
    psum x1, blocking collectives, per_device(): gram_matrix = lax.psum(local_gram, ('ax', 'tr'))  99.3 us
    pad x24, local copies, waits for them, and re-layouts, per_device(): lax.associative_scan(compose, (carry_coef[None], source_terms), axis=1)  60.3 us
    select_n x124, other arithmetic, step(): jnp.where(position < mine, new, old)  54.4 us
    all_gather x1, blocking collectives, prefix(): pieces = jax.tree.map(lambda part: lax.all_gather(part, axis), value)  40.6 us
    dynamic_slice x62, local copies, waits for them, and re-layouts, step(): longer = join(subtotal, jax.tree.map(lambda part: part[position], pieces))  22.2 us
    add x15, other arithmetic, per_device(): lax.associative_scan(compose, (carry_coef[None], source_terms), axis=1)  14.2 us
  transfers between devices with their start and end apart: 2, of which 2 were waited for; matrix products, arithmetic and copies ran while one was open for 0% of the time, Pallas kernels for 0%

commit v1 on v0

v1 whole, which is shorter than its diff:
```python
import functools

import jax
import jax.numpy as jnp
from jax import lax
from jax.experimental import pallas as pl
from jax.experimental.pallas import tpu as pltpu
from jax.sharding import PartitionSpec as P

MESH = pl.DeviceIdType.MESH
F32 = jnp.float32
BF16 = jnp.bfloat16
NS = 64
NZ = 32
NT = 256
LZ, LX, LY = 8, 4, 8
SLICE = NT // LZ


def split(value):
    high = value.astype(BF16)
    low = (value - high.astype(F32)).astype(BF16)
    return high, low


def place():
    ax, tr = lax.axis_index("ax"), lax.axis_index("tr")
    return ax // LZ, lax.rem(ax, LZ), tr // 2, lax.rem(tr, 2)


def device(x, z, y, c):
    return {"ax": x * LZ + z, "tr": y * 2 + c}


def ring(count, body):
    def step(i, carry):
        body(i)
        return carry

    lax.fori_loop(1, count, step, 0)


def await_bytes(ref, sem):
    pltpu.make_async_copy(ref, ref, sem).wait()


def sweep_kernel(
    solid, inlet, ntu, rate,
    gram_out, snap_out,
    xb, ntu_v, rate_v, inlet_v, xs, coef, snap0, ends, snap,
    send_c, send_bu, send_x, send_e, send_g, send_h,
    recv_c, recv_bu, recv_x, recv_e, recv_g, recv_h,
    coef_t, inlet_t, total, load_sem, out_sem, ssem, rsem,
):
    x, z, y, c = place()
    xc = x * 2 + c

    loads = [
        pltpu.make_async_copy(src, dst, load_sem.at[i])
        for i, (src, dst) in enumerate(
            [(ntu, ntu_v), (rate, rate_v), (solid, xb), (inlet, inlet_v)]
        )
    ]
    for load in loads:
        load.start()

    def peer_z(i):
        return lax.rem(z + i, LZ)

    def peer_y(i):
        return lax.rem(y + i, LY)

    def peer_xc(i):
        return lax.rem(xc + i, 2 * LX)

    def dev_z(i):
        return device(x, peer_z(i), y, c)

    def dev_y(i):
        return device(x, z, peer_y(i), c)

    def dev_xc(i):
        p = peer_xc(i)
        return device(p // 2, z, y, lax.rem(p, 2))

    barrier = pltpu.get_barrier_semaphore()
    for count, dev in ((LZ, dev_z), (2 * LX, dev_xc), (LY, dev_y)):
        ring(count, lambda i, dev=dev: pl.semaphore_signal(
            barrier, inc=1, device_id=dev(i), device_id_type=MESH))

    loads[0].wait()
    loads[1].wait()
    n_all = ntu_v[...]
    r_all = rate_v[...]
    a_all = 1.0 / (1.0 + n_all)
    s_all = n_all / (1.0 + n_all)
    coef[0] = a_all.reshape(NZ // 8, 8, NT)
    coef[1] = s_all.reshape(NZ // 8, 8, NT)
    coef[6] = r_all.reshape(NZ // 8, 8, NT)
    sr_all = s_all * r_all
    p = jnp.ones((1, NT), F32)
    q = jnp.zeros((1, NT), F32)
    for k in range(NZ):
        a = a_all[k : k + 1]
        p = a * p
        q = a * q + sr_all[k : k + 1] * p
        coef[2, k // 8, k % 8 : k % 8 + 1, :] = p
        coef[3, k // 8, k % 8 : k % 8 + 1, :] = q
    p_all = coef[2].reshape(NZ, NT)
    q_all = coef[3].reshape(NZ, NT)
    bw = r_all * p_all
    aw = (1.0 - r_all) * bw + r_all * q_all
    coef[4] = bw.reshape(NZ // 8, 8, NT)
    coef[5] = aw.reshape(NZ // 8, 8, NT)
    both = lambda u: jnp.sum(u, axis=0, keepdims=True)
    rows = jnp.concatenate(
        [
            p, q,
            0.5 * both(q_all * q_all + aw * aw),
            both(q_all * p_all + aw * bw),
            0.5 * both(p_all * p_all + bw * bw),
            jnp.zeros((3, NT), F32),
        ],
        axis=0,
    )
    send_c[0] = rows[:, :128]
    send_c[1] = rows[:, 128:]

    loads[2].wait()
    chunk = 16

    def widen(i, carry):
        part = xb[pl.ds(i * 8, 8)].astype(F32)
        for h in range(2):
            xs[h, pl.ds(i * 8 * NZ, 8 * NZ), :] = part[:, :, h * 128 : h * 128 + 128].reshape(8 * NZ, 128)
        return carry

    lax.fori_loop(0, NS // 8, widen, 0)

    def sweep_chunk(ci, carry):
        n0 = ci * chunk

        def plane(kg, i, state):
            new = []
            k = kg * 8 + i
            for h in range(2):
                f1, f2, u1, u2 = state[h]
                lanes = pl.ds(h * 128, 128)
                one = lambda m: jnp.broadcast_to(coef[m, kg, i : i + 1, lanes], (chunk, 128))
                a, s, pp, qq, bb, aa, r = (one(m) for m in range(7))
                v = xs[h, pl.ds(n0 * NZ + k, chunk, stride=NZ), :]
                f1 = a * f1 + s * v
                v = v + r * (f1 - v)
                f2 = a * f2 + s * v
                w = v + r * (f2 - v)
                snap0[k, pl.ds(n0, chunk), lanes] = f2
                snap0[NZ + k, pl.ds(n0, chunk), lanes] = w
                u1 = u1 + (qq * f2 + aa * w)
                u2 = u2 + (pp * f2 + bb * w)
                new.append((f1, f2, u1, u2))
            return tuple(new)

        def planes(kg, state):
            for i in range(8):
                state = plane(kg, i, state)
            return state

        zero = jnp.zeros((chunk, 128), F32)
        state = lax.fori_loop(0, NZ // 8, planes, ((zero,) * 4,) * 2)
        for h in range(2):
            for m in range(4):
                ends[m, pl.ds(n0, chunk), h * 128 : h * 128 + 128] = state[h][m]
        return carry

    lax.fori_loop(0, NS // chunk, sweep_chunk, 0)
    for m in range(2):
        flat = jnp.concatenate([ends[2 * m], ends[2 * m + 1]], axis=0)
        send_bu[m] = flat.T.reshape(LZ, SLICE, 128)

    pl.semaphore_wait(barrier, (LZ - 1) + (2 * LX - 1) + (LY - 1))

    ring(LZ, lambda i: pltpu.make_async_remote_copy(
        send_c.at[peer_z(i) // 4], recv_c.at[z], ssem.at[0], rsem.at[0],
        device_id=dev_z(i), device_id_type=MESH).start())
    for m in range(2):
        ring(LZ, lambda i: pltpu.make_async_remote_copy(
            send_bu.at[m, peer_z(i)], recv_bu.at[m, z], ssem.at[1 + m], rsem.at[1 + m],
            device_id=dev_z(i), device_id_type=MESH).start())
    recv_c[z] = send_c[z // 4]
    recv_bu[0, z] = send_bu[0, z]
    recv_bu[1, z] = send_bu[1, z]

    loads[3].wait()
    inl = inlet_v[...]
    inlet_t[...] = jnp.concatenate([inl, inl], axis=0).T.reshape(LZ, SLICE, 128)

    def inner(k, acc):
        high, low = split(snap0[k])
        rowsb = jnp.concatenate([high, low], axis=0)
        return acc + lax.dot_general(rowsb, rowsb, (((1,), (1,)), ((), ())), preferred_element_type=F32)

    acc = lax.fori_loop(0, 2 * NZ, inner, jnp.zeros((2 * NS, 2 * NS), F32), unroll=4)
    gram0 = (acc[:NS, :NS] + acc[NS:, NS:]) + (acc[:NS, NS:] + acc[NS:, :NS])

    await_bytes(recv_c.at[pl.ds(0, LZ - 1)], rsem.at[0])
    coef_t[...] = recv_c[...].reshape(LZ * 8, 128).T
    ct = coef_t[pl.ds(pl.multiple_of(lax.rem(z, 4) * SLICE, SLICE), SLICE), :]
    lane = lax.broadcasted_iota(jnp.int32, (SLICE, 128), 1)
    second = lane >= NS
    wide = lambda k, m: jnp.broadcast_to(ct[:, k * 8 + m : k * 8 + m + 1], (SLICE, 128))
    turn = lambda u: pltpu.roll(u, NS, 1)
    aks = [wide(k, 0) for k in range(LZ)]
    cks = [wide(k, 1) for k in range(LZ)]
    c2s = [jnp.where(second, ck, 0.0) for ck in cks]
    await_bytes(recv_bu.at[0, pl.ds(0, LZ - 1)], rsem.at[1])
    bks = [recv_bu[0, k] for k in range(LZ)]
    bds = [jnp.where(second, turn(b), b) for b in bks]
    full, dup, at, ctot = bks[0], bds[0], aks[0], cks[0]
    for k in range(1, LZ):
        full, dup = aks[k] * full + c2s[k] * dup + bks[k], aks[k] * dup + bds[k]
        at, ctot = aks[k] * at, aks[k] * ctot + cks[k] * at
    send_x[0] = full
    send_x[1] = jnp.where(second, ctot, at)

    def send_line(i):
        px = lax.rem(x + i, LX)
        pltpu.make_async_remote_copy(
            send_x, recv_x.at[x], ssem.at[3], rsem.at[3],
            device_id=device(px, z, y, c), device_id_type=MESH).start()

    ring(LX, send_line)
    recv_x[x] = send_x[...]
    await_bytes(recv_x.at[pl.ds(0, LX - 1)], rsem.at[3])
    e = inlet_t[z]
    d = e
    for k in range(LX - 1):
        f, cf = recv_x[k, 0], recv_x[k, 1]
        rolled = turn(cf)
        a = jnp.where(second, rolled, cf)
        c2 = jnp.where(second, cf, 0.0)
        fd = jnp.where(second, turn(f), f)
        e_new = a * e + c2 * d + f
        d_new = a * d + fd
        upstream = jnp.full((SLICE, 128), k, jnp.int32) < x
        e = jnp.where(upstream, e_new, e)
        d = jnp.where(upstream, d_new, d)
    for k in range(LZ):
        send_e[k] = e
        if k < LZ - 1:
            e, d = aks[k] * e + c2s[k] * d + bks[k], aks[k] * d + bds[k]
    ring(LZ, lambda i: pltpu.make_async_remote_copy(
        send_e.at[peer_z(i)], recv_e.at[z], ssem.at[4], rsem.at[4],
        device_id=dev_z(i), device_id_type=MESH).start())
    recv_e[z] = send_e[z]

    await_bytes(recv_bu.at[1, pl.ds(0, LZ - 1)], rsem.at[2])
    vs = []
    for k in range(LZ):
        ek = send_e[k]
        hk = jnp.where(second, wide(k, 4), wide(k, 2))
        abk = jnp.where(second, 0.0, wide(k, 3))
        vs.append(recv_bu[1, k] + hk * ek + abk * turn(ek))
    vh, vl = split(jnp.concatenate(vs, axis=0))
    eh, el = split(send_e[...].reshape(LZ * SLICE, 128))
    prod = lax.dot_general(
        jnp.concatenate([vh, vl], axis=1), jnp.concatenate([eh, el], axis=1),
        (((0,), (0,)), ((), ())), preferred_element_type=F32)
    prod = (prod[:128, :128] + prod[128:, 128:]) + (prod[:128, 128:] + prod[128:, :128])
    cross = prod[:NS, :NS] + prod[NS:, NS:]
    gram = gram0 + (cross + cross.T)
    send_g[...] = jnp.concatenate([gram[: NS // 2], gram[NS // 2 :]], axis=1)

    ring(2 * LX, lambda i: pltpu.make_async_remote_copy(
        send_g, recv_g.at[xc], ssem.at[5], rsem.at[5],
        device_id=dev_xc(i), device_id_type=MESH).start())
    recv_g[xc] = send_g[...]
    await_bytes(recv_g.at[pl.ds(0, 2 * LX - 1)], rsem.at[5])

    def add(parts):
        while len(parts) > 1:
            parts = [parts[i] + parts[i + 1] for i in range(0, len(parts), 2)]
        return parts[0]

    sums = add([recv_g[i] for i in range(2 * LX)])
    halves = [sums[:16], sums[16:]]
    for phase in range(2):
        for h in range(2):
            send_h[phase, h] = halves[h]
        for h in range(2):
            over_z = (h + phase) % 2 == 0
            dev, mine = (dev_z, z) if over_z else (dev_y, y)
            slot = 6 + 2 * phase + h
            ring(8, lambda i, dev=dev, mine=mine, slot=slot, h=h: pltpu.make_async_remote_copy(
                send_h.at[phase, h], recv_h.at[phase, h, mine], ssem.at[slot], rsem.at[slot],
                device_id=dev(i), device_id_type=MESH).start())
            recv_h[phase, h, mine] = halves[h]
        if phase == 0:
            await_bytes(recv_e.at[pl.ds(0, LZ - 1)], rsem.at[4])
            ends_t = recv_e[...].reshape(NT, 128).T
            ends[0] = ends_t[:NS]
            ends[1] = ends_t[NS:]

            def finish(kg, carry):
                for i in range(8):
                    k = kg * 8 + i
                    for ph, m1, m2 in ((0, 3, 2), (1, 5, 4)):
                        c1 = coef[m1, kg, i : i + 1, :]
                        c2_ = coef[m2, kg, i : i + 1, :]
                        high, low = split(snap0[ph * NZ + k] + c1 * ends[0] + c2_ * ends[1])
                        snap[ph * NZ + k, :NS, :] = high
                        snap[ph * NZ + k, NS:, :] = low
                return carry

            lax.fori_loop(0, NZ // 8, finish, 0)
            pltpu.make_async_copy(snap, snap_out, out_sem).start()
        for h in range(2):
            slot = 6 + 2 * phase + h
            await_bytes(recv_h.at[phase, h, pl.ds(0, 7)], rsem.at[slot])
        halves = [add([recv_h[phase, h, i] for i in range(8)]) for h in range(2)]
    gram_out[...] = jnp.concatenate(halves, axis=0)

    await_bytes(recv_c.at[pl.ds(0, LZ - 1)], ssem.at[0])
    await_bytes(recv_bu.at[0, pl.ds(0, LZ - 1)], ssem.at[1])
    await_bytes(recv_bu.at[1, pl.ds(0, LZ - 1)], ssem.at[2])
    await_bytes(recv_x.at[pl.ds(0, LX - 1)], ssem.at[3])
    await_bytes(recv_e.at[pl.ds(0, LZ - 1)], ssem.at[4])
    await_bytes(recv_g.at[pl.ds(0, 2 * LX - 1)], ssem.at[5])
    for slot in range(6, 10):
        await_bytes(recv_h.at[0, 0, pl.ds(0, 7)], ssem.at[slot])
    pltpu.make_async_copy(snap, snap_out, out_sem).wait()


def reciprocal(d):
    r = pl.reciprocal(d, approx=True)
    r = r * (2.0 - d * r)
    return r * (2.0 - d * r)


def eliminate(gram):
    rows_i = lax.broadcasted_iota(jnp.int32, (8, 128), 0)
    lane_i = lax.broadcasted_iota(jnp.int32, (8, 128), 1)
    w = []
    for b in range(8):
        part = gram[(b % 4) * 8 : (b % 4) * 8 + 8, :]
        if b >= 4:
            part = pltpu.roll(part, NS, 1)
        eye = (lane_i == rows_i + (NS + 8 * b)).astype(F32)
        w.append(jnp.where(lane_i < NS, part, eye))
    done = []
    for step in range(16):
        b, s0 = divmod(4 * step, 8)
        full = (8, 128)
        r = [jnp.broadcast_to(w[b][s0 + i : s0 + i + 1, :], full) for i in range(4)]
        d = {
            (i, j): jnp.broadcast_to(r[i][:, 4 * step + j : 4 * step + j + 1], full)
            for i in range(4) for j in range(i, 4)
        }
        low, inv, piv = {}, [], []
        for i in range(4):
            inv.append(reciprocal(d[i, i]))
            piv.append(d[i, i])
            for j in range(i + 1, 4):
                low[j, i] = d[i, j] * inv[i]
            for j in range(i + 1, 4):
                for m in range(j, 4):
                    d[j, m] = d[j, m] - low[j, i] * d[i, m]
                r[j] = r[j] - low[j, i] * r[i]
        for i in range(4):
            done.append(r[i] * lax.rsqrt(piv[i]))
        t = [None] * 4
        for i in reversed(range(4)):
            t[i] = inv[i] * r[i]
            for j in range(i + 1, 4):
                t[i] = t[i] - low[j, i] * t[j]
        first = b if s0 == 0 else b + 1
        for g in range(first, 8):
            cols = [jnp.broadcast_to(w[g][:, 4 * step + i : 4 * step + i + 1], full) for i in range(4)]
            w[g] = w[g] - ((cols[0] * t[0] + cols[1] * t[1]) + (cols[2] * t[2] + cols[3] * t[3]))
    out = []
    for b in range(8):
        rows = done[8 * b]
        for s in range(1, 8):
            rows = jnp.where(rows_i == s, done[8 * b + s], rows)
        out.append(rows)
    return jnp.concatenate(out, axis=0)


CHUNKS = 8


def basis_kernel(root, gram, snap_in, basis, factor, snap, out, in_sem, out_sem):
    per = 2 * NZ // CHUNKS
    loads = [
        pltpu.make_async_copy(snap_in.at[pl.ds(i * per, per)], snap.at[pl.ds(i * per, per)], in_sem.at[i])
        for i in range(CHUNKS)
    ]
    for load in loads:
        load.start()
    rows = eliminate(gram)
    upper = lax.broadcasted_iota(jnp.int32, (NS, NS), 1) >= lax.broadcasted_iota(jnp.int32, (NS, NS), 0)
    factor[...] = jnp.where(upper, rows[:, :NS] * (1.0 / root), 0.0)
    high, low = split(rows[:, NS:] * root)
    lhs = jnp.concatenate([high, high, low], axis=1)
    stores = []
    for i in range(CHUNKS):
        loads[i].wait()
        for k in range(i * per, i * per + per):
            both = snap[k]
            rhs = jnp.concatenate([both, both[:NS]], axis=0)
            res = jnp.dot(lhs, rhs, preferred_element_type=F32)
            for h in range(2):
                out[h, pl.ds(k, NS, stride=2 * NZ), :] = res[:, h * 128 : h * 128 + 128]
        ph, z0 = divmod(i * per, NZ)
        for h in range(2):
            copy = pltpu.make_async_copy(
                out.at[h].reshape(NS, 2 * NZ, 128).at[:, pl.ds(i * per, per), :],
                basis.at[:, ph, pl.ds(z0, per), pl.ds(h * 128, 128)], out_sem.at[h, i])
            copy.start()
            stores.append(copy)
    for copy in stores:
        copy.wait()


def per_device(total_rows, solid_start, inlet, ntu, solid_rate):
    vm, dma = pltpu.VMEM, pltpu.SemaphoreType.DMA
    anywhere = pl.BlockSpec(memory_space=pl.ANY)
    invmem = pl.BlockSpec(memory_space=pltpu.VMEM)
    gram, snap = pl.pallas_call(
        sweep_kernel,
        out_shape=(
            jax.ShapeDtypeStruct((32, 128), F32),
            jax.ShapeDtypeStruct((2 * NZ, 2 * NS, NT), BF16),
        ),
        in_specs=[anywhere] * 4,
        out_specs=(invmem, anywhere),
        scratch_shapes=[
            vm((NS, NZ, NT), BF16),
            vm((NZ, NT), F32),
            vm((NZ, NT), F32),
            vm((NS, NT), F32),
            vm((2, NS * NZ, 128), F32),
            vm((7, NZ // 8, 8, NT), F32),
            vm((2 * NZ, NS, NT), F32),
            vm((4, NS, NT), F32),
            vm((2 * NZ, 2 * NS, NT), BF16),
            vm((2, 8, 128), F32),
            vm((2, LZ, SLICE, 128), F32),
            vm((2, SLICE, 128), F32),
            vm((LZ, SLICE, 128), F32),
            vm((32, 128), F32),
            vm((2, 2, 16, 128), F32),
            vm((LZ, 8, 128), F32),
            vm((2, LZ, SLICE, 128), F32),
            vm((LX, 2, SLICE, 128), F32),
            vm((LZ, SLICE, 128), F32),
            vm((2 * LX, 32, 128), F32),
            vm((2, 2, 8, 16, 128), F32),
            vm((128, 64), F32),
            vm((LZ, SLICE, 128), F32),
            vm((8, 128), F32),
            dma((4,)),
            dma,
            dma((10,)),
            dma((10,)),
        ],
        name="sweep",
        compiler_params=pltpu.CompilerParams(
            collective_id=0, has_side_effects=True, vmem_limit_bytes=40 << 20),
    )(solid_start, inlet, ntu, solid_rate)
    root = float(total_rows) ** 0.5
    basis, factor = pl.pallas_call(
        functools.partial(basis_kernel, root),
        out_shape=(
            jax.ShapeDtypeStruct((NS, 2, NZ, NT), F32),
            jax.ShapeDtypeStruct((NS, NS), F32),
        ),
        in_specs=[invmem, anywhere],
        out_specs=(anywhere, invmem),
        scratch_shapes=[
            vm((2 * NZ, 2 * NS, NT), BF16),
            vm((2, NS * 2 * NZ, 128), F32),
            dma((CHUNKS,)),
            dma((2, CHUNKS)),
        ],
        name="basis",
        compiler_params=pltpu.CompilerParams(vmem_limit_bytes=40 << 20),
    )(gram, snap)
    return basis, factor


def solution(mesh):
    placed = (P(None, "ax", "tr"), P(None, "tr"), P("ax", "tr"), P("ax", "tr"))
    total_rows = 2 * NZ * mesh.shape["ax"] * NT * mesh.shape["tr"]
    return jax.shard_map(
        functools.partial(per_device, total_rows),
        mesh=mesh,
        in_specs=placed,
        out_specs=(P(None, None, "ax", "tr"), P()),
        check_vma=False,
    )
```

time: 500 us -> 56.5 us (0.11); the launches traced: 493 us -> 56.2 us
  blocking collectives: 140 us -> 0 us
  waiting for transfers between devices: 124 us -> 0 us
  other arithmetic: 105 us -> 0 us
  local copies, waits for them, and re-layouts: 95 us -> 3.57 us
  Pallas kernels: 0 us -> 52 us
  between operations: 14.9 us -> 0.65 us
  matrix products: 12.1 us -> 0 us
    all_gather x2 -> x0, waiting for transfers between devices: 124 us -> none  [prefix(): pieces = jax.tree.map(lambda part: lax.all_gather(part, axis), value)]
    psum x1 -> x0, blocking collectives: 99.3 us -> none  [per_device(): gram_matrix = lax.psum(local_gram, ('ax', 'tr'))]
    pad x24 -> x0, local copies, waits for them, and re-layouts: 60.3 us -> none  [per_device(): lax.associative_scan(compose, (carry_coef[None], source_terms), axis=1)]
    select_n x124 -> x0, other arithmetic: 54.4 us -> none  [step(): jnp.where(position < mine, new, old)]
    pallas_call x0 -> x2, Pallas kernels: none -> 52 us  [the longest x1 42 us: per_device(): pl.pallas_call(sweep_kernel, out_shape=(jax.ShapeDtypeStruct((32, 128), F...]
    all_gather x1 -> x0, blocking collectives: 40.6 us -> none  [prefix(): pieces = jax.tree.map(lambda part: lax.all_gather(part, axis), value)]
    add x34 -> x0, other arithmetic: 24.1 us -> none  [the longest x15 14.2 us: per_device(): lax.associative_scan(compose, (carry_coef[None], source_terms), axis=1)]
    dynamic_slice x62 -> x0, local copies, waits for them, and re-layouts: 22.2 us -> none  [step(): longer = join(subtotal, jax.tree.map(lambda part: part[position], pieces))]
  transfers between devices with their start and end apart: 2 -> 0, of which waited for: 2 -> 0; matrix products, arithmetic and copies ran while one was open for 0% -> 0% of each run, Pallas kernels for 0% -> 0%
where the time goes in v1:
time: 56.5 us; the launch traced here: 56.2 us
  Pallas kernels  52 us (92%)
  local copies, waits for them, and re-layouts  3.57 us (6%)
  between operations  0.65 us (1%)
    pallas_call x1, Pallas kernels, per_device(): pl.pallas_call(sweep_kernel, out_shape=(jax.ShapeDtypeStruct((32, 128), F...  42 us
    pallas_call x1, Pallas kernels, per_device(): pl.pallas_call(functools.partial(basis_kernel, root), out_shape=(jax.Shap...  9.93 us
    unnamed x8, local copies, waits for them, and re-layouts  3.57 us

profile of v1, /device:TPU:1, one launch (start us, length us, event | category | flops | bytes accessed | tf_op | source)
XLA Modules:
  0.0 56.2 jit_solution(12607213453486261766)
XLA Ops:
  0.6 0.0 copy-start
  0.6 1.2 %copy-done = bf16[64,32,256]{2,1,0:T(8,128)(2,1)S(1)} copy-done((bf16[64,32,256]{2,1,0:T(8,128)(2,1)S(1)}, bf16[64,32,256]{2,1,0:T(8,128)(2,1)}, u32[]{:S(2)}) %copy-start) | copy-done | bytes 1048600
  1.9 0.0 copy-start.1
  1.9 0.8 %copy-done.1 = f32[64,256]{1,0:T(8,128)S(1)} copy-done((f32[64,256]{1,0:T(8,128)S(1)}, f32[64,256]{1,0:T(8,128)}, u32[]{:S(2)}) %copy-start.1) | copy-done | bytes 65560
  2.7 0.0 copy-start.2
  2.7 0.8 %copy-done.2 = f32[32,256]{1,0:T(8,128)S(1)} copy-done((f32[32,256]{1,0:T(8,128)S(1)}, f32[32,256]{1,0:T(8,128)}, u32[]{:S(2)}) %copy-start.2) | copy-done | bytes 32792
  3.5 0.0 copy-start.3
  3.5 0.8 %copy-done.3 = f32[32,256]{1,0:T(8,128)S(1)} copy-done((f32[32,256]{1,0:T(8,128)S(1)}, f32[32,256]{1,0:T(8,128)}, u32[]{:S(2)}) %copy-start.3) | copy-done | bytes 32792
  4.2 42.0 %sweep.1 = (f32[32,128]{1,0:T(8,128)S(1)}, bf16[64,128,256]{2,1,0:T(8,128)(2,1)S(1)}) custom-call(bf16[64,32,256]{2,1,0:T(8,128)(2,1)S(1)} %copy-done, f32[64,256]{1,0:T(8,128)S(1)} %copy-done.1, f32[32,256]{1,0:T(8,128)S(1)} %copy-done.2, f32[32,256]{1,0:T(8,128)S(1)} %copy-done.3), custom_call_target="tpu_custom_call" | custom-call | tf_op jit(solution)/shard_map/sweep/pallas_call | solution.py:428
  46.2 9.9 %basis.1 = (f32[64,2,32,256]{3,2,1,0:T(8,128)}, f32[64,64]{1,0:T(8,128)}) custom-call(f32[32,128]{1,0:T(8,128)S(1)} %get-tuple-element.4.gram, bf16[64,128,256]{2,1,0:T(8,128)(2,1)S(1)} %get-tuple-element.5.snap_in), custom_call_target="tpu_custom_call" | custom-call | tf_op jit(solution)/shard_map/basis/pallas_call | solution.py:471
Async XLA Ops:
  0.6 1.2 %copy-start = (bf16[64,32,256]{2,1,0:T(8,128)(2,1)S(1)}, bf16[64,32,256]{2,1,0:T(8,128)(2,1)}, u32[]{:S(2)}) copy-start(bf16[64,32,256]{2,1,0:T(8,128)(2,1)} %solid.1) | copy-start | bytes 3145732
  1.9 0.8 %copy-start.1 = (f32[64,256]{1,0:T(8,128)S(1)}, f32[64,256]{1,0:T(8,128)}, u32[]{:S(2)}) copy-start(f32[64,256]{1,0:T(8,128)} %inlet.1) | copy-start | bytes 196612
  2.7 0.8 %copy-start.2 = (f32[32,256]{1,0:T(8,128)S(1)}, f32[32,256]{1,0:T(8,128)}, u32[]{:S(2)}) copy-start(f32[32,256]{1,0:T(8,128)} %ntu.1) | copy-start | bytes 98308
  3.5 0.8 %copy-start.3 = (f32[32,256]{1,0:T(8,128)S(1)}, f32[32,256]{1,0:T(8,128)}, u32[]{:S(2)}) copy-start(f32[32,256]{1,0:T(8,128)} %rate.1) | copy-start | bytes 98308

commit v2 on v1

--- a/solution.py
+++ b/solution.py
@@ -33,11 +33,12 @@
 
 
 def ring(count, body):
-    def step(i, carry):
-        body(i)
+    def step(j, carry):
+        away = (j + 1) // 2
+        body(count // 2 + away * (1 - 2 * lax.rem(j + 1, 2)))
         return carry
 
-    lax.fori_loop(1, count, step, 0)
+    lax.fori_loop(0, count - 1, step, 0)
 
 
 def await_bytes(ref, sem):
@@ -46,11 +47,11 @@
 
 def sweep_kernel(
     solid, inlet, ntu, rate,
-    gram_out, snap_out,
-    xb, ntu_v, rate_v, inlet_v, xs, coef, snap0, ends, snap,
+    gram_out, snap,
+    xb, ntu_v, rate_v, inlet_v, xs, coef, snap0, ends,
     send_c, send_bu, send_x, send_e, send_g, send_h,
     recv_c, recv_bu, recv_x, recv_e, recv_g, recv_h,
-    coef_t, inlet_t, total, load_sem, out_sem, ssem, rsem,
+    coef_t, inlet_t, load_sem, ssem, rsem,
 ):
     x, z, y, c = place()
     xc = x * 2 + c
@@ -132,7 +133,9 @@
     def widen(i, carry):
         part = xb[pl.ds(i * 8, 8)].astype(F32)
         for h in range(2):
-            xs[h, pl.ds(i * 8 * NZ, 8 * NZ), :] = part[:, :, h * 128 : h * 128 + 128].reshape(8 * NZ, 128)
+            for g in range(NZ // 8):
+                tile = part[:, g * 8 : g * 8 + 8, h * 128 : h * 128 + 128]
+                xs[h, g, pl.ds(pl.multiple_of(i * 64, 64), 64), :] = tile.reshape(64, 128)
         return carry
 
     lax.fori_loop(0, NS // 8, widen, 0)
@@ -148,7 +151,7 @@
                 lanes = pl.ds(h * 128, 128)
                 one = lambda m: jnp.broadcast_to(coef[m, kg, i : i + 1, lanes], (chunk, 128))
                 a, s, pp, qq, bb, aa, r = (one(m) for m in range(7))
-                v = xs[h, pl.ds(n0 * NZ + k, chunk, stride=NZ), :]
+                v = xs[h, kg, pl.ds(n0 * 8 + i, chunk, stride=8), :]
                 f1 = a * f1 + s * v
                 v = v + r * (f1 - v)
                 f2 = a * f2 + s * v
@@ -312,7 +315,6 @@
                 return carry
 
             lax.fori_loop(0, NZ // 8, finish, 0)
-            pltpu.make_async_copy(snap, snap_out, out_sem).start()
         for h in range(2):
             slot = 6 + 2 * phase + h
             await_bytes(recv_h.at[phase, h, pl.ds(0, 7)], rsem.at[slot])
@@ -327,75 +329,80 @@
     await_bytes(recv_g.at[pl.ds(0, 2 * LX - 1)], ssem.at[5])
     for slot in range(6, 10):
         await_bytes(recv_h.at[0, 0, pl.ds(0, 7)], ssem.at[slot])
-    pltpu.make_async_copy(snap, snap_out, out_sem).wait()
 
 
 def reciprocal(d):
     r = pl.reciprocal(d, approx=True)
-    r = r * (2.0 - d * r)
     return r * (2.0 - d * r)
 
 
+def rsqrt(d):
+    r = lax.rsqrt(d)
+    return r * (1.5 - (0.5 * d * r) * r)
+
+
 def eliminate(gram):
-    rows_i = lax.broadcasted_iota(jnp.int32, (8, 128), 0)
-    lane_i = lax.broadcasted_iota(jnp.int32, (8, 128), 1)
-    w = []
+    full = (8, 128)
+    rows_i = lax.broadcasted_iota(jnp.int32, full, 0)
+    lane_i = lax.broadcasted_iota(jnp.int32, full, 1)
+    left = lane_i < NS
+    w, on_rows, on_lanes = [], [], jnp.zeros(full, F32)
     for b in range(8):
         part = gram[(b % 4) * 8 : (b % 4) * 8 + 8, :]
         if b >= 4:
             part = pltpu.roll(part, NS, 1)
+        diag = jnp.where(lane_i == rows_i + 8 * b, part, 0.0)
+        on_rows.append(jnp.broadcast_to(jnp.sum(diag, axis=1, keepdims=True), full))
+        on_lanes = on_lanes + diag
+        w.append(part)
+    on_lanes = jnp.broadcast_to(jnp.sum(on_lanes, axis=0, keepdims=True), full)
+    on_lanes = jnp.where(left, on_lanes, pltpu.roll(on_lanes, NS, 1))
+    unit = rsqrt(on_lanes)
+    undo = jnp.where(left, on_lanes * unit, unit)
+    for b in range(8):
         eye = (lane_i == rows_i + (NS + 8 * b)).astype(F32)
-        w.append(jnp.where(lane_i < NS, part, eye))
-    done = []
-    for step in range(16):
-        b, s0 = divmod(4 * step, 8)
-        full = (8, 128)
-        r = [jnp.broadcast_to(w[b][s0 + i : s0 + i + 1, :], full) for i in range(4)]
-        d = {
-            (i, j): jnp.broadcast_to(r[i][:, 4 * step + j : 4 * step + j + 1], full)
-            for i in range(4) for j in range(i, 4)
-        }
-        low, inv, piv = {}, [], []
-        for i in range(4):
-            inv.append(reciprocal(d[i, i]))
-            piv.append(d[i, i])
-            for j in range(i + 1, 4):
-                low[j, i] = d[i, j] * inv[i]
-            for j in range(i + 1, 4):
-                for m in range(j, 4):
-                    d[j, m] = d[j, m] - low[j, i] * d[i, m]
-                r[j] = r[j] - low[j, i] * r[i]
-        for i in range(4):
-            done.append(r[i] * lax.rsqrt(piv[i]))
-        t = [None] * 4
-        for i in reversed(range(4)):
-            t[i] = inv[i] * r[i]
-            for j in range(i + 1, 4):
-                t[i] = t[i] - low[j, i] * t[j]
-        first = b if s0 == 0 else b + 1
-        for g in range(first, 8):
-            cols = [jnp.broadcast_to(w[g][:, 4 * step + i : 4 * step + i + 1], full) for i in range(4)]
-            w[g] = w[g] - ((cols[0] * t[0] + cols[1] * t[1]) + (cols[2] * t[2] + cols[3] * t[3]))
+        w[b] = jnp.where(left, w[b] * (rsqrt(on_rows[b]) * unit), eye)
     out = []
     for b in range(8):
-        rows = done[8 * b]
+        r = [jnp.broadcast_to(w[b][i : i + 1, :], full) for i in range(8)]
+        column = lambda u, i: jnp.broadcast_to(u[:, 8 * b + i : 8 * b + i + 1], full)
+        d = {(i, j): column(r[i], j) for i in range(8) for j in range(i, 8)}
+        cols = {g: [column(w[g], i) for i in range(8)] for g in range(b + 1, 8)}
+        done = []
+        for i in range(0, 8, 2):
+            k = i + 1
+            d00, d01, d11 = d[i, i], d[i, k], d[k, k]
+            det = d00 * d11 - d01 * d01
+            inv = reciprocal(det)
+            a00, a01, a11 = d11 * inv, d01 * inv, d00 * inv
+            y = {}
+            for j in range(i + 2, 8):
+                y[j] = (a00 * d[i, j] - a01 * d[k, j], a11 * d[k, j] - a01 * d[i, j])
+            x0 = a00 * r[i] - a01 * r[k]
+            x1 = a11 * r[k] - a01 * r[i]
+            for j in range(i + 2, 8):
+                for m in range(j, 8):
+                    d[j, m] = d[j, m] - (d[i, j] * y[m][0] + d[k, j] * y[m][1])
+                r[j] = r[j] - (d[i, j] * x0 + d[k, j] * x1)
+            for g in range(b + 1, 8):
+                c = cols[g]
+                w[g] = w[g] - (c[i] * x0 + c[k] * x1)
+                for j in range(i + 2, 8):
+                    c[j] = c[j] - (c[i] * y[j][0] + c[k] * y[j][1])
+            done.append(r[i] * rsqrt(d00))
+            done.append((d00 * r[k] - d01 * r[i]) * rsqrt(d00 * det))
+        rows = done[0]
         for s in range(1, 8):
-            rows = jnp.where(rows_i == s, done[8 * b + s], rows)
-        out.append(rows)
+            rows = jnp.where(rows_i == s, done[s], rows)
+        out.append(rows * undo)
     return jnp.concatenate(out, axis=0)
 
 
 CHUNKS = 8
 
 
-def basis_kernel(root, gram, snap_in, basis, factor, snap, out, in_sem, out_sem):
+def basis_kernel(root, gram, snap, basis, factor, out, out_sem):
     per = 2 * NZ // CHUNKS
-    loads = [
-        pltpu.make_async_copy(snap_in.at[pl.ds(i * per, per)], snap.at[pl.ds(i * per, per)], in_sem.at[i])
-        for i in range(CHUNKS)
-    ]
-    for load in loads:
-        load.start()
     rows = eliminate(gram)
     upper = lax.broadcasted_iota(jnp.int32, (NS, NS), 1) >= lax.broadcasted_iota(jnp.int32, (NS, NS), 0)
     factor[...] = jnp.where(upper, rows[:, :NS] * (1.0 / root), 0.0)
@@ -403,22 +410,43 @@
     lhs = jnp.concatenate([high, high, low], axis=1)
     stores = []
     for i in range(CHUNKS):
-        loads[i].wait()
         for k in range(i * per, i * per + per):
             both = snap[k]
             rhs = jnp.concatenate([both, both[:NS]], axis=0)
             res = jnp.dot(lhs, rhs, preferred_element_type=F32)
             for h in range(2):
-                out[h, pl.ds(k, NS, stride=2 * NZ), :] = res[:, h * 128 : h * 128 + 128]
+                out[h, i, pl.ds(k - i * per, NS, stride=8), :] = res[:, h * 128 : h * 128 + 128]
         ph, z0 = divmod(i * per, NZ)
         for h in range(2):
             copy = pltpu.make_async_copy(
-                out.at[h].reshape(NS, 2 * NZ, 128).at[:, pl.ds(i * per, per), :],
+                out.at[h, i].reshape(NS, 8, 128),
                 basis.at[:, ph, pl.ds(z0, per), pl.ds(h * 128, 128)], out_sem.at[h, i])
             copy.start()
             stores.append(copy)
     for copy in stores:
         copy.wait()
+
+
+def basis_call(total_rows, gram, snap):
+    vm, dma = pltpu.VMEM, pltpu.SemaphoreType.DMA
+    anywhere = pl.BlockSpec(memory_space=pl.ANY)
+    invmem = pl.BlockSpec(memory_space=pltpu.VMEM)
+    root = float(total_rows) ** 0.5
+    return pl.pallas_call(
+        functools.partial(basis_kernel, root),
+        out_shape=(
+            jax.ShapeDtypeStruct((NS, 2, NZ, NT), F32),
+            jax.ShapeDtypeStruct((NS, NS), F32),
+        ),
+        in_specs=[invmem, invmem],
+        out_specs=(anywhere, invmem),
+        scratch_shapes=[
+            vm((2, CHUNKS, NS * 8, 128), F32),
+            dma((2, CHUNKS)),
+        ],
+        name="basis",
+        compiler_params=pltpu.CompilerParams(vmem_limit_bytes=40 << 20),
+    )(gram, snap)
 
 
 def per_device(total_rows, solid_start, inlet, ntu, solid_rate):
@@ -431,18 +459,17 @@
             jax.ShapeDtypeStruct((32, 128), F32),
             jax.ShapeDtypeStruct((2 * NZ, 2 * NS, NT), BF16),
         ),
-        in_specs=[anywhere] * 4,
-        out_specs=(invmem, anywhere),
+        in_specs=[pl.BlockSpec(memory_space=pltpu.HBM)] * 4,
+        out_specs=(invmem, invmem),
         scratch_shapes=[
             vm((NS, NZ, NT), BF16),
             vm((NZ, NT), F32),
             vm((NZ, NT), F32),
             vm((NS, NT), F32),
-            vm((2, NS * NZ, 128), F32),
+            vm((2, NZ // 8, NS * 8, 128), F32),
             vm((7, NZ // 8, 8, NT), F32),
             vm((2 * NZ, NS, NT), F32),
             vm((4, NS, NT), F32),
-            vm((2 * NZ, 2 * NS, NT), BF16),
             vm((2, 8, 128), F32),
             vm((2, LZ, SLICE, 128), F32),
             vm((2, SLICE, 128), F32),
@@ -457,34 +484,15 @@
             vm((2, 2, 8, 16, 128), F32),
             vm((128, 64), F32),
             vm((LZ, SLICE, 128), F32),
-            vm((8, 128), F32),
             dma((4,)),
-            dma,
             dma((10,)),
             dma((10,)),
         ],
         name="sweep",
         compiler_params=pltpu.CompilerParams(
             collective_id=0, has_side_effects=True, vmem_limit_bytes=40 << 20),
-    )(solid_start, inlet, ntu, solid_rate)
-    root = float(total_rows) ** 0.5
-    basis, factor = pl.pallas_call(
-        functools.partial(basis_kernel, root),
-        out_shape=(
-            jax.ShapeDtypeStruct((NS, 2, NZ, NT), F32),
-            jax.ShapeDtypeStruct((NS, NS), F32),
-        ),
-        in_specs=[invmem, anywhere],
-        out_specs=(anywhere, invmem),
-        scratch_shapes=[
-            vm((2 * NZ, 2 * NS, NT), BF16),
-            vm((2, NS * 2 * NZ, 128), F32),
-            dma((CHUNKS,)),
-            dma((2, CHUNKS)),
-        ],
-        name="basis",
-        compiler_params=pltpu.CompilerParams(vmem_limit_bytes=40 << 20),
-    )(gram, snap)
+    )(*(pltpu.with_memory_space_constraint(v, pltpu.HBM) for v in (solid_start, inlet, ntu, solid_rate)))
+    basis, factor = basis_call(total_rows, gram, snap)
     return basis, factor
 
 

time: 56.5 us -> 46 us (0.81)
  Pallas kernels: 52 us -> 45.2 us
  local copies, waits for them, and re-layouts: 3.57 us -> 0 us
    pallas_call x1, Pallas kernels: 9.93 us -> 5.29 us  [basis_call(): pl.pallas_call(functools.partial(basis_kernel, root), out_shape=(jax.Shap...]
    unnamed x8 -> x0, local copies, waits for them, and re-layouts: 3.57 us -> none
    pallas_call x1, Pallas kernels: 42 us -> 39.9 us  [per_device(): pl.pallas_call(sweep_kernel, out_shape=(jax.ShapeDtypeStruct((32, 128), F...]
where the time goes in v2:
time: 46 us; the launch traced here: 45.8 us
  Pallas kernels  45.2 us (98%)
  between operations  0.64 us (1%)
    pallas_call x1, Pallas kernels, per_device(): pl.pallas_call(sweep_kernel, out_shape=(jax.ShapeDtypeStruct((32, 128), F...  39.9 us
    pallas_call x1, Pallas kernels, basis_call(): pl.pallas_call(functools.partial(basis_kernel, root), out_shape=(jax.Shap...  5.29 us

profile of v2, /device:TPU:1, one launch (start us, length us, event | category | flops | bytes accessed | tf_op | source)
XLA Modules:
  0.0 45.8 jit_solution(2141508043515295979)
XLA Ops:
  0.6 39.9 %sweep.1 = (f32[32,128]{1,0:T(8,128)S(1)}, bf16[64,128,256]{2,1,0:T(8,128)(2,1)S(1)}) custom-call(bf16[64,32,256]{2,1,0:T(8,128)(2,1)} %solid.1, f32[64,256]{1,0:T(8,128)} %inlet.1, f32[32,256]{1,0:T(8,128)} %ntu.1, f32[32,256]{1,0:T(8,128)} %rate.1), custom_call_target="tpu_custom_call" | custom-call | tf_op jit(solution)/shard_map/sweep/pallas_call | solution.py:456
  40.5 5.3 %basis.1 = (f32[64,2,32,256]{3,2,1,0:T(8,128)}, f32[64,64]{1,0:T(8,128)}) custom-call(f32[32,128]{1,0:T(8,128)S(1)} %get-tuple-element.4.gram, bf16[64,128,256]{2,1,0:T(8,128)(2,1)S(1)} %get-tuple-element.5.snap), custom_call_target="tpu_custom_call" | custom-call | tf_op jit(solution)/shard_map/basis/pallas_call | solution.py:435

commit v3 on v2

--- a/solution.py
+++ b/solution.py
@@ -62,9 +62,6 @@
             [(ntu, ntu_v), (rate, rate_v), (solid, xb), (inlet, inlet_v)]
         )
     ]
-    for load in loads:
-        load.start()
-
     def peer_z(i):
         return lax.rem(z + i, LZ)
 
@@ -85,7 +82,10 @@
         return device(p // 2, z, y, lax.rem(p, 2))
 
     barrier = pltpu.get_barrier_semaphore()
-    for count, dev in ((LZ, dev_z), (2 * LX, dev_xc), (LY, dev_y)):
+    for at, (count, dev) in enumerate(((LZ, dev_z), (2 * LX, dev_xc), (LY, dev_y))):
+        if at == 1:
+            for load in loads:
+                load.start()
         ring(count, lambda i, dev=dev: pl.semaphore_signal(
             barrier, inc=1, device_id=dev(i), device_id_type=MESH))
 
@@ -94,21 +94,29 @@
     n_all = ntu_v[...]
     r_all = rate_v[...]
     a_all = 1.0 / (1.0 + n_all)
-    s_all = n_all / (1.0 + n_all)
-    coef[0] = a_all.reshape(NZ // 8, 8, NT)
-    coef[1] = s_all.reshape(NZ // 8, 8, NT)
+    s_all = n_all * a_all
+    sr_all = s_all * r_all
+    row = lax.broadcasted_iota(jnp.int32, (8, NT), 0)
+    shift = lambda u, k, fill: jnp.where(row >= k, pltpu.roll(u, k, 0), fill)
+    groups = range(NZ // 8)
+    scales = [[a_all[g * 8 : g * 8 + 8]] for g in groups]
+    for k in (1, 2, 4):
+        for scale in scales:
+            scale.append(scale[-1] * shift(scale[-1], k, 1.0))
+    p_all, q_all = [], []
+    for g in groups:
+        p_all.append(scales[g][3] * p_all[-1][7:8] if g else scales[g][3])
+        q = sr_all[g * 8 : g * 8 + 8] * p_all[g]
+        for step, k in enumerate((1, 2, 4)):
+            q = q + scales[g][step] * shift(q, k, 0.0)
+        q_all.append(q)
+    for g in groups[1:]:
+        q_all[g] = q_all[g] + scales[g][3] * q_all[g - 1][7:8]
+    p, q = p_all[-1][7:8], q_all[-1][7:8]
+    p_all, q_all = jnp.concatenate(p_all, axis=0), jnp.concatenate(q_all, axis=0)
+    for m, u in enumerate((a_all, s_all, p_all, q_all)):
+        coef[m] = u.reshape(NZ // 8, 8, NT)
     coef[6] = r_all.reshape(NZ // 8, 8, NT)
-    sr_all = s_all * r_all
-    p = jnp.ones((1, NT), F32)
-    q = jnp.zeros((1, NT), F32)
-    for k in range(NZ):
-        a = a_all[k : k + 1]
-        p = a * p
-        q = a * q + sr_all[k : k + 1] * p
-        coef[2, k // 8, k % 8 : k % 8 + 1, :] = p
-        coef[3, k // 8, k % 8 : k % 8 + 1, :] = q
-    p_all = coef[2].reshape(NZ, NT)
-    q_all = coef[3].reshape(NZ, NT)
     bw = r_all * p_all
     aw = (1.0 - r_all) * bw + r_all * q_all
     coef[4] = bw.reshape(NZ // 8, 8, NT)
@@ -212,32 +220,78 @@
     second = lane >= NS
     wide = lambda k, m: jnp.broadcast_to(ct[:, k * 8 + m : k * 8 + m + 1], (SLICE, 128))
     turn = lambda u: pltpu.roll(u, NS, 1)
+    first = lambda u: jnp.where(second, 0.0, u)
     aks = [wide(k, 0) for k in range(LZ)]
     cks = [wide(k, 1) for k in range(LZ)]
     c2s = [jnp.where(second, ck, 0.0) for ck in cks]
+    at, ctot = aks[0], cks[0]
+    reach = [None]
+    for k in range(1, LZ):
+        reach.append((at, ctot))
+        at, ctot = aks[k] * at, aks[k] * ctot + cks[k] * at
+    send_x[1] = jnp.where(second, ctot, at)
+
+    def send_line(part):
+        def send(i):
+            px = lax.rem(x + i, LX)
+            pltpu.make_async_remote_copy(
+                send_x.at[part], recv_x.at[part, x], ssem.at[3 + 8 * part], rsem.at[3 + 8 * part],
+                device_id=device(px, z, y, c), device_id_type=MESH).start()
+
+        ring(LX, send)
+        recv_x[part, x] = send_x[part]
+
+    send_line(1)
     await_bytes(recv_bu.at[0, pl.ds(0, LZ - 1)], rsem.at[1])
     bks = [recv_bu[0, k] for k in range(LZ)]
     bds = [jnp.where(second, turn(b), b) for b in bks]
-    full, dup, at, ctot = bks[0], bds[0], aks[0], cks[0]
+    full, dup = bks[0], bds[0]
+    before = [None]
     for k in range(1, LZ):
+        before.append((full,) + reach[k])
         full, dup = aks[k] * full + c2s[k] * dup + bks[k], aks[k] * dup + bds[k]
-        at, ctot = aks[k] * at, aks[k] * ctot + cks[k] * at
     send_x[0] = full
-    send_x[1] = jnp.where(second, ctot, at)
-
-    def send_line(i):
-        px = lax.rem(x + i, LX)
-        pltpu.make_async_remote_copy(
-            send_x, recv_x.at[x], ssem.at[3], rsem.at[3],
-            device_id=device(px, z, y, c), device_id_type=MESH).start()
-
-    ring(LX, send_line)
-    recv_x[x] = send_x[...]
-    await_bytes(recv_x.at[pl.ds(0, LX - 1)], rsem.at[3])
+    send_line(0)
+
+    aas, abs_, bbs = ([wide(k, m) for k in range(LZ)] for m in (2, 3, 4))
+    aa, ab, bb = aas[0], abs_[0], bbs[0]
+    for k in range(1, LZ):
+        _, ah, ch = before[k]
+        a2 = ah * ah
+        ac = ah * ch
+        aa = aa + (aas[k] * a2 + abs_[k] * ac + bbs[k] * (ch * ch))
+        ab = ab + (abs_[k] * a2 + 2.0 * bbs[k] * ac)
+        bb = bb + bbs[k] * a2
+    await_bytes(recv_bu.at[1, pl.ds(0, LZ - 1)], rsem.at[2])
+    answer = recv_bu[1, 0]
+    vs = []
+    for k in range(1, LZ):
+        e0, ah, ch = before[k]
+        te = turn(e0)
+        own = jnp.where(second, bbs[k], aas[k]) * e0
+        u = recv_bu[1, k]
+        vs.append(u + own + first(abs_[k]) * te)
+        w = u + 2.0 * own + abs_[k] * te
+        answer = answer + (ah * w + first(ch) * turn(w))
+
+    def cross(v, e):
+        vh, vl = split(v)
+        eh, el = split(e)
+        prod = lax.dot_general(
+            jnp.concatenate([vh, vl], axis=1), jnp.concatenate([eh, el], axis=1),
+            (((0,), (0,)), ((), ())), preferred_element_type=F32)
+        prod = (prod[:128, :128] + prod[128:, 128:]) + (prod[:128, 128:] + prod[128:, :128])
+        part = prod[:NS, :NS] + prod[NS:, NS:]
+        return part + part.T
+
+    gram1 = gram0 + cross(
+        jnp.concatenate(vs, axis=0), jnp.concatenate([before[k][0] for k in range(1, LZ)], axis=0))
+    for part in range(2):
+        await_bytes(recv_x.at[part, pl.ds(0, LX - 1)], rsem.at[3 + 8 * part])
     e = inlet_t[z]
     d = e
     for k in range(LX - 1):
-        f, cf = recv_x[k, 0], recv_x[k, 1]
+        f, cf = recv_x[0, k], recv_x[1, k]
         rolled = turn(cf)
         a = jnp.where(second, rolled, cf)
         c2 = jnp.where(second, cf, 0.0)
@@ -247,6 +301,13 @@
         upstream = jnp.full((SLICE, 128), k, jnp.int32) < x
         e = jnp.where(upstream, e_new, e)
         d = jnp.where(upstream, d_new, d)
+    gram = gram1 + cross(answer + jnp.where(second, bb, aa) * e + first(ab) * turn(e), e)
+    send_g[...] = jnp.concatenate([gram[: NS // 2], gram[NS // 2 :]], axis=1)
+
+    ring(2 * LX, lambda i: pltpu.make_async_remote_copy(
+        send_g, recv_g.at[xc], ssem.at[5], rsem.at[5],
+        device_id=dev_xc(i), device_id_type=MESH).start())
+
     for k in range(LZ):
         send_e[k] = e
         if k < LZ - 1:
@@ -255,27 +316,6 @@
         send_e.at[peer_z(i)], recv_e.at[z], ssem.at[4], rsem.at[4],
         device_id=dev_z(i), device_id_type=MESH).start())
     recv_e[z] = send_e[z]
-
-    await_bytes(recv_bu.at[1, pl.ds(0, LZ - 1)], rsem.at[2])
-    vs = []
-    for k in range(LZ):
-        ek = send_e[k]
-        hk = jnp.where(second, wide(k, 4), wide(k, 2))
-        abk = jnp.where(second, 0.0, wide(k, 3))
-        vs.append(recv_bu[1, k] + hk * ek + abk * turn(ek))
-    vh, vl = split(jnp.concatenate(vs, axis=0))
-    eh, el = split(send_e[...].reshape(LZ * SLICE, 128))
-    prod = lax.dot_general(
-        jnp.concatenate([vh, vl], axis=1), jnp.concatenate([eh, el], axis=1),
-        (((0,), (0,)), ((), ())), preferred_element_type=F32)
-    prod = (prod[:128, :128] + prod[128:, 128:]) + (prod[:128, 128:] + prod[128:, :128])
-    cross = prod[:NS, :NS] + prod[NS:, NS:]
-    gram = gram0 + (cross + cross.T)
-    send_g[...] = jnp.concatenate([gram[: NS // 2], gram[NS // 2 :]], axis=1)
-
-    ring(2 * LX, lambda i: pltpu.make_async_remote_copy(
-        send_g, recv_g.at[xc], ssem.at[5], rsem.at[5],
-        device_id=dev_xc(i), device_id_type=MESH).start())
     recv_g[xc] = send_g[...]
     await_bytes(recv_g.at[pl.ds(0, 2 * LX - 1)], rsem.at[5])
 
@@ -289,15 +329,18 @@
     for phase in range(2):
         for h in range(2):
             send_h[phase, h] = halves[h]
+        def send_halves(i):
+            for h in range(2):
+                over_z = (h + phase) % 2 == 0
+                dev, mine, slot = dev_z(i) if over_z else dev_y(i), z if over_z else y, 6 + 2 * phase + h
+                pltpu.make_async_remote_copy(
+                    send_h.at[phase, h], recv_h.at[phase, h, mine], ssem.at[slot], rsem.at[slot],
+                    device_id=dev, device_id_type=MESH).start()
+
+        ring(8, send_halves)
         for h in range(2):
-            over_z = (h + phase) % 2 == 0
-            dev, mine = (dev_z, z) if over_z else (dev_y, y)
-            slot = 6 + 2 * phase + h
-            ring(8, lambda i, dev=dev, mine=mine, slot=slot, h=h: pltpu.make_async_remote_copy(
-                send_h.at[phase, h], recv_h.at[phase, h, mine], ssem.at[slot], rsem.at[slot],
-                device_id=dev(i), device_id_type=MESH).start())
-            recv_h[phase, h, mine] = halves[h]
-        if phase == 0:
+            recv_h[phase, h, z if (h + phase) % 2 == 0 else y] = halves[h]
+        if phase == 1:
             await_bytes(recv_e.at[pl.ds(0, LZ - 1)], rsem.at[4])
             ends_t = recv_e[...].reshape(NT, 128).T
             ends[0] = ends_t[:NS]
@@ -324,7 +367,8 @@
     await_bytes(recv_c.at[pl.ds(0, LZ - 1)], ssem.at[0])
     await_bytes(recv_bu.at[0, pl.ds(0, LZ - 1)], ssem.at[1])
     await_bytes(recv_bu.at[1, pl.ds(0, LZ - 1)], ssem.at[2])
-    await_bytes(recv_x.at[pl.ds(0, LX - 1)], ssem.at[3])
+    for part in range(2):
+        await_bytes(recv_x.at[part, pl.ds(0, LX - 1)], ssem.at[3 + 8 * part])
     await_bytes(recv_e.at[pl.ds(0, LZ - 1)], ssem.at[4])
     await_bytes(recv_g.at[pl.ds(0, 2 * LX - 1)], ssem.at[5])
     for slot in range(6, 10):
@@ -478,15 +522,15 @@
             vm((2, 2, 16, 128), F32),
             vm((LZ, 8, 128), F32),
             vm((2, LZ, SLICE, 128), F32),
-            vm((LX, 2, SLICE, 128), F32),
+            vm((2, LX, SLICE, 128), F32),
             vm((LZ, SLICE, 128), F32),
             vm((2 * LX, 32, 128), F32),
             vm((2, 2, 8, 16, 128), F32),
             vm((128, 64), F32),
             vm((LZ, SLICE, 128), F32),
             dma((4,)),
-            dma((10,)),
-            dma((10,)),
+            dma((12,)),
+            dma((12,)),
         ],
         name="sweep",
         compiler_params=pltpu.CompilerParams(

time: 46 us -> 45.1 us (0.980)
  Pallas kernels: 45.2 us -> 44 us
    pallas_call x1, Pallas kernels: 39.9 us -> 38.8 us  [per_device(): pl.pallas_call(sweep_kernel, out_shape=(jax.ShapeDtypeStruct((32, 128), F...]
where the time goes in v3:
time: 45.1 us; the launch traced here: 44.7 us
  Pallas kernels  44 us (98%)
  between operations  0.64 us (1%)
    pallas_call x1, Pallas kernels, per_device(): pl.pallas_call(sweep_kernel, out_shape=(jax.ShapeDtypeStruct((32, 128), F...  38.8 us
    pallas_call x1, Pallas kernels, basis_call(): pl.pallas_call(functools.partial(basis_kernel, root), out_shape=(jax.Shap...  5.29 us

profile of v3, /device:TPU:1, one launch (start us, length us, event | category | flops | bytes accessed | tf_op | source)
XLA Modules:
  0.0 44.7 jit_solution(7532834527276302722)
XLA Ops:
  0.6 38.8 %sweep.1 = (f32[32,128]{1,0:T(8,128)S(1)}, bf16[64,128,256]{2,1,0:T(8,128)(2,1)S(1)}) custom-call(bf16[64,32,256]{2,1,0:T(8,128)(2,1)} %solid.1, f32[64,256]{1,0:T(8,128)} %inlet.1, f32[32,256]{1,0:T(8,128)} %ntu.1, f32[32,256]{1,0:T(8,128)} %rate.1), custom_call_target="tpu_custom_call" | custom-call | tf_op jit(solution)/shard_map/sweep/pallas_call | solution.py:500
  39.4 5.3 %basis.1 = (f32[64,2,32,256]{3,2,1,0:T(8,128)}, f32[64,64]{1,0:T(8,128)}) custom-call(f32[32,128]{1,0:T(8,128)S(1)} %get-tuple-element.4.gram, bf16[64,128,256]{2,1,0:T(8,128)(2,1)S(1)} %get-tuple-element.5.snap), custom_call_target="tpu_custom_call" | custom-call | tf_op jit(solution)/shard_map/basis/pallas_call | solution.py:479

commit v4 on v3

--- a/solution.py
+++ b/solution.py
@@ -49,8 +49,8 @@
     solid, inlet, ntu, rate,
     gram_out, snap,
     xb, ntu_v, rate_v, inlet_v, xs, coef, snap0, ends,
-    send_c, send_bu, send_x, send_e, send_g, send_h,
-    recv_c, recv_bu, recv_x, recv_e, recv_g, recv_h,
+    send_c, send_bu, send_x, send_e, send_g, send_h, send_d,
+    recv_c, recv_bu, recv_x, recv_e, recv_g, recv_h, recv_d,
     coef_t, inlet_t, load_sem, ssem, rsem,
 ):
     x, z, y, c = place()
@@ -193,7 +193,7 @@
     ring(LZ, lambda i: pltpu.make_async_remote_copy(
         send_c.at[peer_z(i) // 4], recv_c.at[z], ssem.at[0], rsem.at[0],
         device_id=dev_z(i), device_id_type=MESH).start())
-    for m in range(2):
+    for m in (0,):
         ring(LZ, lambda i: pltpu.make_async_remote_copy(
             send_bu.at[m, peer_z(i)], recv_bu.at[m, z], ssem.at[1 + m], rsem.at[1 + m],
             device_id=dev_z(i), device_id_type=MESH).start())
@@ -211,6 +211,10 @@
         return acc + lax.dot_general(rowsb, rowsb, (((1,), (1,)), ((), ())), preferred_element_type=F32)
 
     acc = lax.fori_loop(0, 2 * NZ, inner, jnp.zeros((2 * NS, 2 * NS), F32), unroll=4)
+    for m in (1,):
+        ring(LZ, lambda i: pltpu.make_async_remote_copy(
+            send_bu.at[m, peer_z(i)], recv_bu.at[m, z], ssem.at[1 + m], rsem.at[1 + m],
+            device_id=dev_z(i), device_id_type=MESH).start())
     gram0 = (acc[:NS, :NS] + acc[NS:, NS:]) + (acc[:NS, NS:] + acc[NS:, :NS])
 
     await_bytes(recv_c.at[pl.ds(0, LZ - 1)], rsem.at[0])
@@ -302,11 +306,21 @@
         e = jnp.where(upstream, e_new, e)
         d = jnp.where(upstream, d_new, d)
     gram = gram1 + cross(answer + jnp.where(second, bb, aa) * e + first(ab) * turn(e), e)
-    send_g[...] = jnp.concatenate([gram[: NS // 2], gram[NS // 2 :]], axis=1)
-
-    ring(2 * LX, lambda i: pltpu.make_async_remote_copy(
-        send_g, recv_g.at[xc], ssem.at[5], rsem.at[5],
-        device_id=dev_xc(i), device_id_type=MESH).start())
+    half = NS // 2
+    down = lax.broadcasted_iota(jnp.int32, (half, half), 0)
+    over = lax.broadcasted_iota(jnp.int32, (half, half), 1)
+    far = gram[half:, half:]
+    square = jnp.concatenate([jnp.where(over >= down, gram[:half, :half], far), gram[:half, half:]], axis=1)
+    send_g[...] = jnp.concatenate([square[:16], square[16:]], axis=1)
+    diag = jnp.sum(jnp.where(over == down, far, 0.0), axis=0, keepdims=True)
+    send_d[0] = jnp.concatenate([diag, jnp.zeros((1, 128 - half), F32)], axis=1)
+
+    def send_sum(i):
+        for src, dst, slot in ((send_g, recv_g.at[xc], 5), (send_d.at[0], recv_d.at[0, xc], 10)):
+            pltpu.make_async_remote_copy(
+                src, dst, ssem.at[slot], rsem.at[slot], device_id=dev_xc(i), device_id_type=MESH).start()
+
+    ring(2 * LX, send_sum)
 
     for k in range(LZ):
         send_e[k] = e
@@ -317,7 +331,9 @@
         device_id=dev_z(i), device_id_type=MESH).start())
     recv_e[z] = send_e[z]
     recv_g[xc] = send_g[...]
+    recv_d[0, xc] = send_d[0]
     await_bytes(recv_g.at[pl.ds(0, 2 * LX - 1)], rsem.at[5])
+    await_bytes(recv_d.at[0, pl.ds(0, 7)], rsem.at[10])
 
     def add(parts):
         while len(parts) > 1:
@@ -325,10 +341,11 @@
         return parts[0]
 
     sums = add([recv_g[i] for i in range(2 * LX)])
-    halves = [sums[:16], sums[16:]]
+    halves = [sums[:8], sums[8:], add([recv_d[0, i] for i in range(2 * LX)])]
     for phase in range(2):
         for h in range(2):
             send_h[phase, h] = halves[h]
+        send_d[1 + phase] = halves[2]
         def send_halves(i):
             for h in range(2):
                 over_z = (h + phase) % 2 == 0
@@ -336,8 +353,13 @@
                 pltpu.make_async_remote_copy(
                     send_h.at[phase, h], recv_h.at[phase, h, mine], ssem.at[slot], rsem.at[slot],
                     device_id=dev, device_id_type=MESH).start()
+            dev, mine = (dev_y(i), y) if phase else (dev_z(i), z)
+            pltpu.make_async_remote_copy(
+                send_d.at[1 + phase], recv_d.at[1 + phase, mine], ssem.at[12 + phase], rsem.at[12 + phase],
+                device_id=dev, device_id_type=MESH).start()
 
         ring(8, send_halves)
+        recv_d[1 + phase, y if phase else z] = halves[2]
         for h in range(2):
             recv_h[phase, h, z if (h + phase) % 2 == 0 else y] = halves[h]
         if phase == 1:
@@ -361,8 +383,15 @@
         for h in range(2):
             slot = 6 + 2 * phase + h
             await_bytes(recv_h.at[phase, h, pl.ds(0, 7)], rsem.at[slot])
+        await_bytes(recv_d.at[1 + phase, pl.ds(0, 7)], rsem.at[12 + phase])
         halves = [add([recv_h[phase, h, i] for i in range(8)]) for h in range(2)]
-    gram_out[...] = jnp.concatenate(halves, axis=0)
+        halves.append(add([recv_d[1 + phase, i] for i in range(8)]))
+    square = jnp.concatenate(halves[:2], axis=0)
+    square = jnp.concatenate([square[:, :NS], square[:, NS:]], axis=0)
+    near, side = square[:, :half], square[:, half:]
+    flip = near.T
+    far = jnp.where(over < down, near, jnp.where(over == down, halves[2][:, :half], flip))
+    gram_out[...] = jnp.concatenate([jnp.where(over >= down, near, flip), side, side.T, far], axis=1)
 
     await_bytes(recv_c.at[pl.ds(0, LZ - 1)], ssem.at[0])
     await_bytes(recv_bu.at[0, pl.ds(0, LZ - 1)], ssem.at[1])
@@ -371,6 +400,8 @@
         await_bytes(recv_x.at[part, pl.ds(0, LX - 1)], ssem.at[3 + 8 * part])
     await_bytes(recv_e.at[pl.ds(0, LZ - 1)], ssem.at[4])
     await_bytes(recv_g.at[pl.ds(0, 2 * LX - 1)], ssem.at[5])
+    for slot in (10, 12, 13):
+        await_bytes(recv_d.at[0, pl.ds(0, 7)], ssem.at[slot])
     for slot in range(6, 10):
         await_bytes(recv_h.at[0, 0, pl.ds(0, 7)], ssem.at[slot])
 
@@ -518,19 +549,21 @@
             vm((2, LZ, SLICE, 128), F32),
             vm((2, SLICE, 128), F32),
             vm((LZ, SLICE, 128), F32),
-            vm((32, 128), F32),
-            vm((2, 2, 16, 128), F32),
+            vm((16, 128), F32),
+            vm((2, 2, 8, 128), F32),
+            vm((3, 1, 128), F32),
             vm((LZ, 8, 128), F32),
             vm((2, LZ, SLICE, 128), F32),
             vm((2, LX, SLICE, 128), F32),
             vm((LZ, SLICE, 128), F32),
-            vm((2 * LX, 32, 128), F32),
-            vm((2, 2, 8, 16, 128), F32),
+            vm((2 * LX, 16, 128), F32),
+            vm((2, 2, 8, 8, 128), F32),
+            vm((3, 8, 1, 128), F32),
             vm((128, 64), F32),
             vm((LZ, SLICE, 128), F32),
             dma((4,)),
-            dma((12,)),
-            dma((12,)),
+            dma((14,)),
+            dma((14,)),
         ],
         name="sweep",
         compiler_params=pltpu.CompilerParams(

time: 45.1 us -> 44.2 us (0.980)
  Pallas kernels: 44 us -> 43.4 us
    pallas_call x1, Pallas kernels: 38.8 us -> 38.1 us  [per_device(): pl.pallas_call(sweep_kernel, out_shape=(jax.ShapeDtypeStruct((32, 128), F...]
where the time goes in v4:
time: 44.2 us; the launch traced here: 44 us
  Pallas kernels  43.4 us (98%)
  between operations  0.64 us (1%)
    pallas_call x1, Pallas kernels, per_device(): pl.pallas_call(sweep_kernel, out_shape=(jax.ShapeDtypeStruct((32, 128), F...  38.1 us
    pallas_call x1, Pallas kernels, basis_call(): pl.pallas_call(functools.partial(basis_kernel, root), out_shape=(jax.Shap...  5.29 us

profile of v4, /device:TPU:1, one launch (start us, length us, event | category | flops | bytes accessed | tf_op | source)
XLA Modules:
  0.0 44.0 jit_solution(16620632489303963894)
XLA Ops:
  0.6 38.1 %sweep.1 = (f32[32,128]{1,0:T(8,128)S(1)}, bf16[64,128,256]{2,1,0:T(8,128)(2,1)S(1)}) custom-call(bf16[64,32,256]{2,1,0:T(8,128)(2,1)} %solid.1, f32[64,256]{1,0:T(8,128)} %inlet.1, f32[32,256]{1,0:T(8,128)} %ntu.1, f32[32,256]{1,0:T(8,128)} %rate.1), custom_call_target="tpu_custom_call" | custom-call | tf_op jit(solution)/shard_map/sweep/pallas_call | solution.py:531
  38.8 5.3 %basis.1 = (f32[64,2,32,256]{3,2,1,0:T(8,128)}, f32[64,64]{1,0:T(8,128)}) custom-call(f32[32,128]{1,0:T(8,128)S(1)} %get-tuple-element.4.gram, bf16[64,128,256]{2,1,0:T(8,128)(2,1)S(1)} %get-tuple-element.5.snap), custom_call_target="tpu_custom_call" | custom-call | tf_op jit(solution)/shard_map/basis/pallas_call | solution.py:510

commit v5 on v4

--- a/solution.py
+++ b/solution.py
@@ -437,7 +437,6 @@
     for b in range(8):
         eye = (lane_i == rows_i + (NS + 8 * b)).astype(F32)
         w[b] = jnp.where(left, w[b] * (rsqrt(on_rows[b]) * unit), eye)
-    out = []
     for b in range(8):
         r = [jnp.broadcast_to(w[b][i : i + 1, :], full) for i in range(8)]
         column = lambda u, i: jnp.broadcast_to(u[:, 8 * b + i : 8 * b + i + 1], full)
@@ -466,11 +465,12 @@
                     c[j] = c[j] - (c[i] * y[j][0] + c[k] * y[j][1])
             done.append(r[i] * rsqrt(d00))
             done.append((d00 * r[k] - d01 * r[i]) * rsqrt(d00 * det))
+            if i < 6:
+                yield None
         rows = done[0]
         for s in range(1, 8):
             rows = jnp.where(rows_i == s, done[s], rows)
-        out.append(rows * undo)
-    return jnp.concatenate(out, axis=0)
+        yield rows * undo
 
 
 CHUNKS = 8
@@ -478,26 +478,47 @@
 
 def basis_kernel(root, gram, snap, basis, factor, out, out_sem):
     per = 2 * NZ // CHUNKS
-    rows = eliminate(gram)
-    upper = lax.broadcasted_iota(jnp.int32, (NS, NS), 1) >= lax.broadcasted_iota(jnp.int32, (NS, NS), 0)
-    factor[...] = jnp.where(upper, rows[:, :NS] * (1.0 / root), 0.0)
-    high, low = split(rows[:, NS:] * root)
-    lhs = jnp.concatenate([high, high, low], axis=1)
+    half = NS // 2
     stores = []
-    for i in range(CHUNKS):
-        for k in range(i * per, i * per + per):
-            both = snap[k]
-            rhs = jnp.concatenate([both, both[:NS]], axis=0)
-            res = jnp.dot(lhs, rhs, preferred_element_type=F32)
+
+    def operand(rows, first, depth):
+        high, low = split(rows[:, NS : NS + depth] * root)
+        return first, depth, jnp.concatenate([high, high, low], axis=1)
+
+    def multiply(i, first, depth, lhs, begin=0, end=per):
+        for k in range(i * per + begin, i * per + end):
+            high, low = snap[k, :depth, :], snap[k, NS : NS + depth, :]
+            res = jnp.dot(lhs, jnp.concatenate([high, low, high], axis=0), preferred_element_type=F32)
             for h in range(2):
-                out[h, i, pl.ds(k - i * per, NS, stride=8), :] = res[:, h * 128 : h * 128 + 128]
+                out[h, i, pl.ds(8 * first + k - i * per, half, stride=8), :] = res[:, h * 128 : h * 128 + 128]
+        if end < per:
+            return
         ph, z0 = divmod(i * per, NZ)
         for h in range(2):
             copy = pltpu.make_async_copy(
-                out.at[h, i].reshape(NS, 8, 128),
-                basis.at[:, ph, pl.ds(z0, per), pl.ds(h * 128, 128)], out_sem.at[h, i])
+                out.at[h, i, pl.ds(8 * first, 8 * half)].reshape(half, 8, 128),
+                basis.at[pl.ds(first, half), ph, pl.ds(z0, per), pl.ds(h * 128, 128)],
+                out_sem.at[h, i, first // half])
             copy.start()
             stores.append(copy)
+
+    rows, turns, top = [], 0, None
+    for block in eliminate(gram):
+        if block is not None:
+            rows.append(block)
+            if len(rows) == 4:
+                top = operand(jnp.concatenate(rows, axis=0), 0, half)
+                continue
+        if top is not None:
+            begin = (turns % 2) * (per // 2)
+            multiply(turns // 2, *top, begin, begin + per // 2)
+            turns += 1
+    rows = jnp.concatenate(rows, axis=0)
+    bottom = operand(rows[half:], half, NS)
+    for i in range(CHUNKS):
+        multiply(i, *bottom)
+    upper = lax.broadcasted_iota(jnp.int32, (NS, NS), 1) >= lax.broadcasted_iota(jnp.int32, (NS, NS), 0)
+    factor[...] = jnp.where(upper, rows[:, :NS] * (1.0 / root), 0.0)
     for copy in stores:
         copy.wait()
 
@@ -517,7 +538,7 @@
         out_specs=(anywhere, invmem),
         scratch_shapes=[
             vm((2, CHUNKS, NS * 8, 128), F32),
-            dma((2, CHUNKS)),
+            dma((2, CHUNKS, 2)),
         ],
         name="basis",
         compiler_params=pltpu.CompilerParams(vmem_limit_bytes=40 << 20),

time: 44.2 us -> 44.1 us (level)
  no operation moved by 1% of the time
where the time goes in v5:
time: 44.1 us; the launch traced here: 44 us
  Pallas kernels  43.3 us (98%)
  between operations  0.64 us (1%)
    pallas_call x1, Pallas kernels, per_device(): pl.pallas_call(sweep_kernel, out_shape=(jax.ShapeDtypeStruct((32, 128), F...  38.1 us
    pallas_call x1, Pallas kernels, basis_call(): pl.pallas_call(functools.partial(basis_kernel, root), out_shape=(jax.Shap...  5.21 us

profile of v5, /device:TPU:1, one launch (start us, length us, event | category | flops | bytes accessed | tf_op | source)
XLA Modules:
  0.0 44.0 jit_solution(1361553862750359826)
XLA Ops:
  0.6 38.1 %sweep.1 = (f32[32,128]{1,0:T(8,128)S(1)}, bf16[64,128,256]{2,1,0:T(8,128)(2,1)S(1)}) custom-call(bf16[64,32,256]{2,1,0:T(8,128)(2,1)} %solid.1, f32[64,256]{1,0:T(8,128)} %inlet.1, f32[32,256]{1,0:T(8,128)} %ntu.1, f32[32,256]{1,0:T(8,128)} %rate.1), custom_call_target="tpu_custom_call" | custom-call | tf_op jit(solution)/shard_map/sweep/pallas_call | solution.py:552
  38.8 5.2 %basis.1 = (f32[64,2,32,256]{3,2,1,0:T(8,128)}, f32[64,64]{1,0:T(8,128)}) custom-call(f32[32,128]{1,0:T(8,128)S(1)} %get-tuple-element.4.gram, bf16[64,128,256]{2,1,0:T(8,128)(2,1)S(1)} %get-tuple-element.5.snap), custom_call_target="tpu_custom_call" | custom-call | tf_op jit(solution)/shard_map/basis/pallas_call | solution.py:531
